TPU v7x, 256 devices: a whole 4x4x8 slice. The times are simulated.
256 devices in a mesh: replica: 16 (over z_hi, x, core), fsdp: 16 (over y, z_lo).
Axes of the slice: x: 4, y: 4, z: 8 (z_hi: 2, z_lo: 4; z = z_hi * 4 + z_lo), core: 2. Of those that a mesh axis runs over, the one named last changes fastest.
Arguments:
- pre_act: bfloat16 [16, 2048, 14336], P('replica', 'fsdp'), may hold values from -6 to 6
- out_grad: bfloat16 [16, 2048, 4096], P('replica', 'fsdp'), may hold values from -0.3125 to 0.3125
- pseudo_grads: float32 [16, 16, 65536], P('replica', 'fsdp'), may hold values from -6 to 6
- outer_params: float32 [16, 65536], P('fsdp'), may hold values from -4 to 4
- momentum: float32 [16, 65536], P('fsdp', 'replica'), may hold values from -6 to 6
Outputs:
- weight_grad: bfloat16 [16, 14336, 4096], P('replica', 'fsdp')
- new_moment: float32 [16, 65536], P('fsdp', 'replica')
- new_params: float32 [16, 65536], P('fsdp')
All inputs are finite; a program needn't handle non-finite values.
Results may differ from a plain program's by a relative error of at most 0.01.
Values may be sent and summed in bfloat16 or wider, within the bound.
No kernel may reach another device: no remote copies, remote signals or barrier semaphores. Data moves between devices by JAX's collectives and lax.ppermute only.
A program may use at most 128 MiB of HBM per device.

v0:
```python
import jax
import jax.numpy as jnp
from jax import lax
from jax.sharding import PartitionSpec as P

outer_mu = 0.9
outer_lr = 0.7


def outer_sync(pseudo_grads, outer_params, momentum):
    pieces = pseudo_grads.reshape(-1)
    replicas = lax.axis_size("replica")
    share = momentum.shape[1]
    position = lax.axis_index("replica") * share
    shard_sum = lax.psum_scatter(
        pieces.astype(jnp.bfloat16), "replica", scatter_dimension=0, tiled=True
    ).astype(jnp.float32)
    delta = shard_sum / replicas
    moment_new = outer_mu * momentum[0] + delta
    old_slice = lax.dynamic_slice_in_dim(outer_params[0], position, share, 0)
    updated = old_slice - outer_lr * (delta + outer_mu * moment_new)
    params_new = lax.all_gather(updated, "replica", axis=0, tiled=True)
    return (moment_new[None], params_new[None])


def weight_gradient(pre_act, out_grad):
    hidden = pre_act[0]
    incoming = out_grad[0]
    unit_block = lax.all_to_all(hidden, "fsdp", split_axis=1, concat_axis=0, tiled=True)
    activated = jax.nn.silu(unit_block.astype(jnp.float32)).astype(jnp.bfloat16)
    summed = lax.dot_general(
        activated,
        lax.all_gather(incoming, "fsdp", axis=0, tiled=True),
        (((0,), (0,)), ((), ())),
        preferred_element_type=jnp.float32,
    )
    return summed.astype(jnp.bfloat16)[None]


def on_device(pre_act, out_grad, pseudo_grads, outer_params, momentum):
    weight_grad = weight_gradient(pre_act, out_grad)
    moment_new, params_new = outer_sync(pseudo_grads, outer_params, momentum)
    return (weight_grad, moment_new, params_new)


def solution(mesh):
    placed = (
        P("replica", "fsdp", None),
        P("replica", "fsdp", None),
        P("replica", "fsdp", None),
        P("fsdp", None),
        P("fsdp", "replica"),
    )
    return jax.shard_map(
        on_device,
        mesh=mesh,
        in_specs=placed,
        out_specs=(P("replica", "fsdp", None), P("fsdp", "replica"), P("fsdp", None)),
        check_vma=False,
    )
```

profile of v0, /device:TPU:67, one launch (start us, length us, event | category | flops | bytes accessed | tf_op | source)
XLA Modules:
  0.0 528.4 jit_solution(11372038130784884745)
XLA Ops:
  8.0 0.0 copy-start
  8.0 0.0 all-reduce.3.cloned.1.call-start
  8.1 2.3 convert_reduce_fusion
  10.4 0.0 all-reduce.3.cloned.1.call-update
  10.4 0.0 all-gather.3.cloned.1.call-start
  10.4 0.5 all-gather.3.cloned.1.call-update
  11.0 0.0 copy-start.2
  11.0 0.0 copy-start.1
  11.0 6.1 %copy.10 = bf16[1,128,14336]{1,2,0:T(8,128)(2,1)} copy(bf16[1,128,14336]{2,1,0:T(8,128)(2,1)} %param.5) | data formatting | bytes 7340032 | tf_op args[0]
  17.1 7.6 %all-to-all-start = ((bf16[128,16,896]{0,2,1:T(8,128)(2,1)}), bf16[128,16,896]{0,2,1:T(8,128)(2,1)}, u32[]{:S(2)}, u32[]{:S(2)}) async-start(bf16[128,16,896]{0,2,1:T(8,128)(2,1)} %bitcast.29), calls=%async_computation | async-start | bytes 7340032 | tf_op jit(solution)/shard_map/all_to_all | solution.py:29
  24.7 0.0 copy-done.2
  24.7 0.6 dynamic-slice.1
  25.9 0.0 copy-done
  26.0 0.0 copy-done.1
  26.0 412.1 %all-reduce.3.cloned.1.call-done = bf16[65536]{0:T(1024)(128)(2,1)} async-done(((bf16[65536]{0:T(1024)(128)(2,1)}), bf16[65536]{0:T(1024)(128)(2,1)}) %all-reduce.3.cloned.1.call-update) | async-done | bytes 131088
  438.1 1.3 multiply_subtract_fusion
  439.4 37.6 %all_gather.7 = f32[65536]{0:T(1024)S(1)} all-gather(f32[4096]{0:T(1024)S(1)} %get-tuple-element.3), channel_id=1, replica_groups=mesh['replica'=16,'fsdp'=16] {'replica'}, dimensions={0}, use_global_device_ids=true | all-gather | bytes 278528 | tf_op jit(solution)/shard_map/all_gather | solution.py:22
  476.9 0.0 all-to-all-done
  476.9 5.8 %convert_bitcast_fusion = f32[16,128,896]{1,2,0:T(8,128)} fusion(bf16[128,16,896]{0,2,1:T(8,128)(2,1)} %all-to-all-done), kind=kLoop, calls=%fused_computation.7 | loop fusion | flops 1835008 | bytes 11010048 | tf_op jit(solution)/shard_map/convert_element_type | solution.py:30
  482.8 8.6 %copy.11 = f32[16,128,896]{2,1,0:T(8,128)} copy(f32[16,128,896]{1,2,0:T(8,128)} %convert_bitcast_fusion) | data formatting | bytes 14680064 | tf_op jit(solution)/shard_map/convert_element_type | solution.py:30
  491.3 6.9 %fusion.5 = bf16[2048,896]{1,0:T(8,128)(2,1)} fusion(f32[16,128,896]{2,1,0:T(8,128)} %copy.11), kind=kLoop, calls=%fused_computation.9 | loop fusion | flops 9175040 | bytes 11010048 | tf_op jit(solution)/shard_map/convert_element_type | solution.py:30
  498.2 0.0 all-gather.3.cloned.1.call-done
  498.2 22.0 %convert_bitcast_fusion.1 = bf16[1,896,4096]{2,1,0:T(8,128)(2,1)} fusion(bf16[2048,896]{1,0:T(8,128)(2,1)} %fusion.5, bf16[1,2048,4096]{2,1,0:T(8,128)(2,1)} %all-gather.3.cloned.1.call-done), kind=kOutput, calls=%fused_computation.8 | convolution fusion | flops 15036055552 | bytes 27787264 | tf_op jit(solution)/shard_map/dot_general | solution.py:31
  520.2 0.7 copy.14
  (2 shorter events, 0.0 us)
Async XLA Ops:
  8.0 17.9 %copy-start = (f32[1,65536]{1,0:T(1,128)S(1)}, f32[1,65536]{1,0:T(1,128)}, u32[]{:S(2)}) copy-start(f32[1,65536]{1,0:T(1,128)} %param.8) | copy-start | bytes 786436
  8.0 430.0 %all-reduce.3.cloned.1.call-start = ((), (), s32[]{:S(2)}) async-start(), calls=%async_computation.2 | async-start | bytes 262144
  10.4 487.8 %all-gather.3.cloned.1.call-start = ((), (), s32[]{:S(2)}) async-start(), calls=%async_computation.1 | async-start | bytes 17825792 | tf_op jit(solution)/shard_map/all_gather | solution.py:33
  11.0 13.7 %copy-start.2 = (u32[256]{0:T(256)S(1)}, u32[256]{0:T(256)}, u32[]{:S(2)}) copy-start(u32[256]{0:T(256)} %constant.29) | copy-start | bytes 3076
  11.0 15.0 %copy-start.1 = (f32[1,4096]{1,0:T(1,128)S(1)}, f32[1,4096]{1,0:T(1,128)}, u32[]{:S(2)}) copy-start(f32[1,4096]{1,0:T(1,128)} %param.9) | copy-start | bytes 49156
  17.1 459.9 %all-to-all-start = ((bf16[128,16,896]{0,2,1:T(8,128)(2,1)}), bf16[128,16,896]{0,2,1:T(8,128)(2,1)}, u32[]{:S(2)}, u32[]{:S(2)}) async-start(bf16[128,16,896]{0,2,1:T(8,128)(2,1)} %bitcast.29), calls=%async_computation | async-start | bytes 7340032 | tf_op jit(solution)/shard_map/all_to_all | solution.py:29
Sparse Core Ops, SparseCore 0:
  12.0 425.9 all-reduce.2
Sparse Core Ops, SparseCore 1:
  12.7 430.0 all-gather.2
where the time goes:
time: 529 us; the launch traced here: 528 us
  waiting for transfers between devices  413 us (78%)
  blocking collectives  37.6 us (7%)
  matrix products  22 us (4%)
  other arithmetic  16.4 us (3%)
  between operations  16.2 us (3%)
  local copies, waits for them, and re-layouts  16 us (3%)
  starting transfers between devices  7.72 us (1%)
    unnamed x3, waiting for transfers between devices  413 us
    all_gather x1, blocking collectives, outer_sync(): params_new = lax.all_gather(updated, 'replica', axis=0, tiled=True)  37.6 us
    dot_general x1, matrix products, weight_gradient(): lax.dot_general(activated, lax.all_gather(incoming, 'fsdp', axis=0, tiled...  22 us
    convert_element_type x2, other arithmetic, weight_gradient(): activated = jax.nn.silu(unit_block.astype(jnp.float32)).astype(jnp.bfloat16)  12.7 us
  transfers between devices with their start and end apart: 3, of which 1 were waited for; matrix products, arithmetic and copies ran while one was open for 6% of the time, Pallas kernels for 0%

commit v1 on v0

v1 whole, which is shorter than its diff:
```python
import jax
import jax.numpy as jnp
from jax import lax
from jax.experimental import pallas as pl
from jax.experimental.pallas import tpu as pltpu
from jax.sharding import PartitionSpec as P

outer_mu = 0.9
outer_lr = 0.7

NY, NZ = 4, 4
COLUMNS = 4096
UNITS = 896
TOK = 128
LANES = 128
REPLICAS = 16
VMEM = 18 * 1024 * 1024


def shift(dy, dz):
    return [
        (y * NZ + z, (y + dy) % NY * NZ + (z + dz) % NZ)
        for y in range(NY)
        for z in range(NZ)
    ]


def fsdp_send(array, dy, dz):
    return lax.ppermute(array, "fsdp", shift(dy, dz))


def activate_kernel(place_ref, *refs):
    for source, target in zip(refs[:NY], refs[NY:]):
        value = source[0].astype(jnp.float32)
        value = value / (1.0 + jnp.exp(-value))
        target[0] = value.T.astype(jnp.bfloat16)


def activate(pre_act, place):
    def column(d):
        return lambda j, p: (0, 0, (p[0] + d) % NY * NZ + (p[1] + j) % NZ)

    return pl.pallas_call(
        activate_kernel,
        grid_spec=pltpu.PrefetchScalarGridSpec(
            num_scalar_prefetch=1,
            grid=(NZ,),
            in_specs=[pl.BlockSpec((1, TOK, UNITS), column(d)) for d in range(NY)],
            out_specs=[
                pl.BlockSpec((1, UNITS, TOK), lambda j, p: (j, 0, 0))
                for _ in range(NY)
            ],
        ),
        out_shape=[jax.ShapeDtypeStruct((NZ, UNITS, TOK), jnp.bfloat16)] * NY,
        compiler_params=pltpu.CompilerParams(vmem_limit_bytes=VMEM),
    )(place, *[pre_act] * NY)


def matmul_kernel(lefts, rights, total, out_ref, packed):
    @pl.when(pl.program_id(0) == 0)
    def _():
        for i, source in enumerate(lefts):
            packed[:, i * TOK : (i + 1) * TOK] = source[0]

    right = jnp.concatenate([r[0] for r in rights], axis=0)
    value = jnp.dot(packed[...], right, preferred_element_type=jnp.float32)
    if total is not None:
        value = value + total[0]
    out_ref[0] = value.astype(out_ref.dtype)


def matmul(blocks, token, total=None, final=False, width=512):
    lefts = [(array, row) for array, row, _ in blocks]
    rights = [r for _, _, parts in blocks for r in parts]
    n, m, depth = len(lefts), len(rights), len(lefts) * TOK
    tile = pl.BlockSpec((1, UNITS, width), lambda i: (0, 0, i))
    operands = [a for a, _ in lefts] + rights + [token]
    in_specs = [
        pl.BlockSpec((1, UNITS, TOK), lambda i, row=row: (row, 0, 0)) for _, row in lefts
    ]
    in_specs += [pl.BlockSpec((1, r.shape[1], width), lambda i: (0, 0, i)) for r in rights]
    in_specs += [pl.BlockSpec(memory_space=pl.ANY)]
    alias = {}
    if total is not None:
        operands.append(total)
        in_specs.append(tile)
        if not final:
            alias = {n + m + 1: 0}

    def kernel(*refs):
        out_ref, token_ref, packed = refs[-3:]
        extra = refs[n + m + 1] if total is not None else None
        matmul_kernel(refs[:n], refs[n : n + m], extra, out_ref, packed)
        token_ref[...] = jnp.zeros_like(token_ref)

    return pl.pallas_call(
        kernel,
        grid=(COLUMNS // width,),
        in_specs=in_specs,
        out_specs=[tile, pl.BlockSpec((8, LANES), lambda i: (0, 0))],
        out_shape=[
            jax.ShapeDtypeStruct(
                (1, UNITS, COLUMNS), jnp.bfloat16 if final else jnp.float32
            ),
            jax.ShapeDtypeStruct((8, LANES), jnp.float32),
        ],
        input_output_aliases=alias,
        scratch_shapes=[pltpu.VMEM((UNITS, depth), jnp.bfloat16)],
        compiler_params=pltpu.CompilerParams(vmem_limit_bytes=VMEM),
        cost_estimate=pl.CostEstimate(
            flops=2 * UNITS * COLUMNS * depth,
            bytes_accessed=UNITS * COLUMNS * 4 + depth * (COLUMNS + UNITS) * 2,
            transcendentals=0,
        ),
    )(*operands)


def reduce_shares(pseudo_grads):
    pieces = pseudo_grads.reshape(REPLICAS, 32, LANES)
    return lax.all_to_all(pieces, "replica", 0, 0, tiled=True)


def outer_update(pieces, outer_params, momentum):
    share = momentum.shape[1]
    index = lax.axis_index("replica")
    delta = jnp.sum(pieces, axis=0).reshape(-1) / REPLICAS
    moment = outer_mu * momentum[0] + delta
    old = lax.dynamic_slice_in_dim(outer_params[0], index * share, share, 0)
    return moment, old - outer_lr * (delta + outer_mu * moment)


def hand_out(updated):
    copies = jnp.broadcast_to(updated.reshape(1, 32, LANES), (REPLICAS, 32, LANES))
    return lax.all_to_all(copies, "replica", 0, 0, tiled=True)


def on_device(pre_act, out_grad, pseudo_grads, outer_params, momentum):
    fsdp = lax.axis_index("fsdp")
    place = jnp.stack([fsdp // NZ, fsdp % NZ]).astype(jnp.int32)
    env = {"b0": out_grad, "token": jnp.zeros((8, LANES), jnp.float32)}

    def past(*values):
        env["token"], *values = lax.optimization_barrier((env["token"], *values))
        return values

    def event(done, start):
        sources = [make() for _, make, _, _ in start]
        held = past(*sources, *[env[name] for name in done])
        env.update(zip(done, held[len(sources) :]))
        for (name, _, dy, dz), source in zip(start, held):
            env[name] = fsdp_send(source, dy, dz)

    def up(k):
        return (f"p{k}", lambda: env[f"b{k}"], 1, 0)

    def down(k):
        return (f"m{k}", lambda: env[f"b{k}"], -1, 0)

    def far(k, step):
        return (f"f{k}", lambda: env[("p" if step > 0 else "m") + str(k)], step, 0)

    def along(k):
        return (f"b{k}", lambda: env[f"b{k - 1}"], 0, 1)

    def spread(s):
        return (f"X{s}", lambda: jnp.stack([env[f"R{d}"][s] for d in every]), 0, s)

    def compute(name, pairs, total=None, final=False):
        blocks = []
        for k, d in pairs:
            array, row = (env[f"R{d}"], 0) if k == 0 else (env[f"X{k}"], d)
            names = [("b", "p", "f", "m")[d] + str(k)]
            right = [env[part] for part in names]
            blocks.append((array, row, right))
        env[name], env["token"] = matmul(blocks, env["token"], total, final)

    every = range(NY)
    event([], [along(1), down(0), up(0)])
    (held,) = past(pre_act)
    env["R0"], env["o1"], env["o2"], env["o3"] = activate(held, place)
    event(
        [],
        [("q2", lambda: env["o2"], 1, 0), ("R3", lambda: env["o3"], -1, 0)],
    )
    event(["b1"], [along(2)])
    env["shares"] = reduce_shares(*past(pseudo_grads))
    event(["p0", "m0"], [("R1", lambda: env["o1"], 1, 0), far(0, -1)])
    event(["b2"], [along(3)])
    event(["q2", "R3"], [("R2", lambda: env["q2"], 1, 0), down(1)])
    event(["R1", "f0", "shares"], [up(1), down(2)])
    moment, updated = outer_update(env["shares"], outer_params, momentum)
    event(["R2", "m1", "b3"], [up(2), far(1, -1), spread(1)])
    env["params"] = hand_out(*past(updated))
    event(["p1", "m2", "X1"], [up(3), down(3), spread(2)])
    event(["p2", "f1", "params"], [far(2, 1)])
    compute("t1", [(k, d) for k in (0, 1) for d in every])
    event(["X2"], [spread(3)])
    event(["m3"], [far(3, -1)])
    compute("t2", [(2, d) for d in (0, 1, 3)], env["t1"])
    event(["p3", "f2", "X3", "f3"], [])
    compute("out", [(2, 2), (3, 0), (3, 1), (3, 2), (3, 3)], env["t2"], final=True)
    return env["out"], moment[None], env["params"].reshape(1, -1)


def solution(mesh):
    placed = (
        P("replica", "fsdp", None),
        P("replica", "fsdp", None),
        P("replica", "fsdp", None),
        P("fsdp", None),
        P("fsdp", "replica"),
    )
    return jax.shard_map(
        on_device,
        mesh=mesh,
        in_specs=placed,
        out_specs=(P("replica", "fsdp", None), P("fsdp", "replica"), P("fsdp", None)),
        check_vma=False,
    )
```

time: 529 us -> 204 us (0.39)
  the two profiles are of different devices: /device:TPU:67 before, /device:TPU:224 now
where the time goes in v1:
time: 204 us; the launch traced here: 200 us
  waiting for transfers between devices  86.6 us (42%)
  starting transfers between devices  53.8 us (26%)
  Pallas kernels  36 us (18%)
  local copies, waits for them, and re-layouts  14.5 us (7%)
  other arithmetic  8.6 us (4%)
    ppermute x22, waiting for transfers between devices, fsdp_send(): return lax.ppermute(array, 'fsdp', shift(dy, dz))  86.6 us
    ppermute x22, starting transfers between devices, fsdp_send(): return lax.ppermute(array, 'fsdp', shift(dy, dz))  34.4 us
    pallas_call x3, Pallas kernels, matmul(): pl.pallas_call(kernel, grid=(COLUMNS // width,), in_specs=in_specs, out_s...  31.4 us
    all_to_all x1, starting transfers between devices, reduce_shares(): return lax.all_to_all(pieces, 'replica', 0, 0, tiled=True)  9.68 us
    all_to_all x1, starting transfers between devices, hand_out(): return lax.all_to_all(copies, 'replica', 0, 0, tiled=True)  9.68 us
    slice x5, local copies, waits for them, and re-layouts, spread(): return (f'X{s}', lambda: jnp.stack([env[f'R{d}'][s] for d in every]), 0, s)  6.86 us
    another operation x3, other arithmetic, spread(): return (f'X{s}', lambda: jnp.stack([env[f'R{d}'][s] for d in every]), 0, s)  6.42 us
    unnamed x17, local copies, waits for them, and re-layouts  6.34 us
  transfers between devices with their start and end apart: 24, of which 15 were waited for; matrix products, arithmetic and copies ran while one was open for 8% of the time, Pallas kernels for 13%

profile of v1, /device:TPU:224, one launch (start us, length us, event | category | flops | bytes accessed | tf_op | source)
XLA Modules:
  0.0 200.2 jit_solution(16865073760220447101)
XLA Ops:
  0.6 0.0 copy-start
  0.6 2.0 collective-permute-start
  2.6 3.0 %collective-permute-start.1 = (bf16[1,128,4096]{2,1,0:T(8,128)(2,1)}, bf16[1,128,4096]{2,1,0:T(8,128)(2,1)}, u32[]{:S(2)}, u32[]{:S(2)}) collective-permute-start(bf16[1,128,4096]{2,1,0:T(8,128)(2,1)} %refs_8_.1), channel_id=1, source_target_pairs={{0,12},{1,13},{2,14},{3,15},{4,0},{5,1},{6,2},{7,3},{8,4},{9,5},{1... | collective-permute-start | bytes 3145736 | tf_op jit(solution)/shard_map/ppermute | solution.py:29
  5.6 0.0 collective-permute-start.2
  5.6 0.1 pad_add_fusion.place_ref
  5.7 2.0 %copy-done.1 = bf16[1,128,14336]{2,1,0:T(8,128)(2,1)S(1)} copy-done((bf16[1,128,14336]{2,1,0:T(8,128)(2,1)S(1)}, bf16[1,128,14336]{2,1,0:T(8,128)(2,1)}, u32[]{:S(2)}) %copy-start.1) | copy-done | bytes 3670040
  7.8 4.6 %shard_map.76 = (bf16[4,896,128]{2,1,0:T(8,128)(2,1)S(1)}, bf16[4,896,128]{2,1,0:T(8,128)(2,1)}, bf16[4,896,128]{2,1,0:T(8,128)(2,1)}, bf16[4,896,128]{2,1,0:T(8,128)(2,1)}) custom-call(s32[2]{0:T(128)S(1)} %pad_add_fusion.place_ref, bf16[1,128,14336]{2,1,0:T(8,128)(2,1)S(1)} %copy-done.1, bf16[1,128,14336]{2,1,0:T(8,128)(2,1)S(1)} %copy-done.1, ...), custom_call_target="tpu_custom_call" | custom-call | tf_op jit(solution)/shard_map/pallas_call | solution.py:43
  12.4 13.6 %collective-permute-done.refs_12_ = bf16[1,128,4096]{2,1,0:T(8,128)(2,1)} collective-permute-done((bf16[1,128,4096]{2,1,0:T(8,128)(2,1)}, bf16[1,128,4096]{2,1,0:T(8,128)(2,1)}, u32[]{:S(2)}, u32[]{:S(2)}) %collective-permute-start) | collective-permute-done | bytes 1048608 | tf_op jit(solution)/shard_map/ppermute | solution.py:29
  25.9 3.7 %collective-permute-start.3 = (bf16[1,128,4096]{2,1,0:T(8,128)(2,1)}, bf16[1,128,4096]{2,1,0:T(8,128)(2,1)S(1)}, u32[]{:S(2)}, u32[]{:S(2)}) collective-permute-start(bf16[1,128,4096]{2,1,0:T(8,128)(2,1)} %collective-permute-done.refs_12_), channel_id=1, source_target_pairs={{0,1},{1,2},{2,3},{3,0},{4,5},{5,6},{6,7},{7,4},{8,9},{9,10},{10,1... | collective-permute-start | bytes 3145736 | tf_op jit(solution)/shard_map/ppermute | solution.py:29
  29.6 1.6 collective-permute-start.4
  31.2 1.7 collective-permute-start.5
  32.9 0.0 collective-permute-done.1.refs_11_
  32.9 0.0 collective-permute-done.2.refs_9_
  32.9 1.8 collective-permute-start.7
  34.7 0.2 collective-permute-start.6
  34.9 9.7 %all-to-all-start = ((f32[16,32,128]{2,1,0:T(8,128)}), f32[16,32,128]{2,1,0:T(8,128)S(1)}, u32[]{:S(2)}, u32[]{:S(2)}) async-start(f32[16,32,128]{2,1,0:T(8,128)} %bitcast.20), calls=%async_computation | async-start | bytes 524288 | tf_op jit(solution)/shard_map/all_to_all | solution.py:120
  44.6 0.6 constant_dynamic-slice_fusion
  45.2 8.0 %collective-permute-done.3.refs_3_ = bf16[1,128,4096]{2,1,0:T(8,128)(2,1)S(1)} collective-permute-done((bf16[1,128,4096]{2,1,0:T(8,128)(2,1)}, bf16[1,128,4096]{2,1,0:T(8,128)(2,1)S(1)}, u32[]{:S(2)}, u32[]{:S(2)}) %collective-permute-start.3) | collective-permute-done | bytes 1048608 | tf_op jit(solution)/shard_map/ppermute | solution.py:29
  53.2 1.2 collective-permute-done.4
  54.4 0.3 collective-permute-done.5.refs_3_
  54.7 1.6 collective-permute-start.9
  56.3 2.2 %collective-permute-start.8 = (bf16[1,128,4096]{2,1,0:T(8,128)(2,1)}, bf16[1,128,4096]{2,1,0:T(8,128)(2,1)}, u32[]{:S(2)}, u32[]{:S(2)}) collective-permute-start(bf16[1,128,4096]{2,1,0:T(8,128)(2,1)} %collective-permute-done.refs_12_), channel_id=1, source_target_pairs={{0,12},{1,13},{2,14},{3,15},{4,0},{5,1},{6,2},{7,3},{8,4},{9,5},{1... | collective-permute-start | bytes 3145736 | tf_op jit(solution)/shard_map/ppermute | solution.py:29
  58.5 2.7 %collective-permute-start.10 = (bf16[1,128,4096]{2,1,0:T(8,128)(2,1)S(1)}, bf16[1,128,4096]{2,1,0:T(8,128)(2,1)S(1)}, u32[]{:S(2)}, u32[]{:S(2)}) collective-permute-start(bf16[1,128,4096]{2,1,0:T(8,128)(2,1)S(1)} %collective-permute-done.3.refs_3_), channel_id=1, source_target_pairs={{0,1},{1,2},{2,3},{3,0},{4,5},{5,6},{6,7},{7,4},{8,9},{9,10},{10,1... | collective-permute-start | bytes 3145736 | tf_op jit(solution)/shard_map/ppermute | solution.py:29
  61.2 0.9 fusion.4
  62.1 0.0 all-to-all-done
  62.1 12.0 %collective-permute-done.6.refs_1_ = bf16[4,896,128]{2,1,0:T(8,128)(2,1)} collective-permute-done((bf16[4,896,128]{2,1,0:T(8,128)(2,1)}, bf16[4,896,128]{2,1,0:T(8,128)(2,1)}, u32[]{:S(2)}, u32[]{:S(2)}) %collective-permute-start.6) | collective-permute-done | bytes 917536 | tf_op jit(solution)/shard_map/ppermute | solution.py:29
  74.1 3.2 %collective-permute-done.7.refs_10_ = bf16[1,128,4096]{2,1,0:T(8,128)(2,1)} collective-permute-done((bf16[1,128,4096]{2,1,0:T(8,128)(2,1)}, bf16[1,128,4096]{2,1,0:T(8,128)(2,1)}, u32[]{:S(2)}, u32[]{:S(2)}) %collective-permute-start.7) | collective-permute-done | bytes 1048608 | tf_op jit(solution)/shard_map/ppermute | solution.py:29
  77.3 1.7 collective-permute-start.11
  79.0 1.7 collective-permute-start.12
  80.6 2.0 fusion.5
  82.6 2.0 fusion.7
  84.6 9.2 %collective-permute-done.9.refs_2_ = bf16[4,896,128]{2,1,0:T(8,128)(2,1)} collective-permute-done((bf16[4,896,128]{2,1,0:T(8,128)(2,1)}, bf16[4,896,128]{2,1,0:T(8,128)(2,1)}, u32[]{:S(2)}, u32[]{:S(2)}) %collective-permute-start.9) | collective-permute-done | bytes 917536 | tf_op jit(solution)/shard_map/ppermute | solution.py:29
  93.8 1.0 slice.48
  94.7 2.0 %pad_maximum_fusion = bf16[4,896,128]{2,1,0:T(8,128)(2,1)} fusion(bf16[1,896,128]{2,1,0:T(8,128)(2,1)S(1)} %get-tuple-element.159, bf16[1,896,128]{2,1,0:T(8,128)(2,1)S(1)} %slice.48, bf16[1,896,128]{2,1,0:T(8,128)(2,1)S(1)} %get-tuple-element.154, bf16[1,896,128]{2,1,0:T(8,128)(2,1)} %get-tuple-element.151), kind=kLoop, calls=%fused_computation | loop fusion | flops 1376256 | bytes 1835008 | tf_op jit(solution)/shard_map/stack | solution.py:166
  96.7 3.0 %collective-permute-done.8.refs_15_ = bf16[1,128,4096]{2,1,0:T(8,128)(2,1)} collective-permute-done((bf16[1,128,4096]{2,1,0:T(8,128)(2,1)}, bf16[1,128,4096]{2,1,0:T(8,128)(2,1)}, u32[]{:S(2)}, u32[]{:S(2)}) %collective-permute-start.8) | collective-permute-done | bytes 1048608 | tf_op jit(solution)/shard_map/ppermute | solution.py:29
  99.8 0.0 collective-permute-done.10.refs_6_
  99.8 0.0 collective-permute-start.13
  99.8 1.6 collective-permute-start.14
  101.3 1.7 collective-permute-start.15
  103.0 1.4 fusion.3
  104.4 0.7 fusion.2
  105.1 0.7 broadcast_in_dim.13
  105.8 9.7 %all-to-all-start.1 = ((f32[16,32,128]{2,1,0:T(8,128)}), f32[16,32,128]{2,1,0:T(8,128)S(1)}, u32[]{:S(2)}, u32[]{:S(2)}) async-start(f32[16,32,128]{2,1,0:T(8,128)} %broadcast_in_dim.13), calls=%async_computation.1 | async-start | bytes 524288 | tf_op jit(solution)/shard_map/all_to_all | solution.py:134
  115.5 1.1 fusion.6
  116.6 2.2 %pad_maximum_fusion.1 = bf16[4,896,128]{2,1,0:T(8,128)(2,1)} fusion(bf16[1,896,128]{2,1,0:T(8,128)(2,1)} %get-tuple-element.158, bf16[1,896,128]{2,1,0:T(8,128)(2,1)S(1)} %get-tuple-element.156, bf16[1,896,128]{2,1,0:T(8,128)(2,1)} %get-tuple-element.153, bf16[1,896,128]{2,1,0:T(8,128)(2,1)} %get-tuple-element.150), kind=kLoop, calls=%fused_computation.1 | loop fusion | flops 1376256 | bytes 1835008 | tf_op jit(solution)/shard_map/stack | solution.py:166
  118.8 0.0 collective-permute-done.11.refs_13_
  118.8 3.4 %collective-permute-done.12.refs_5_ = bf16[1,128,4096]{2,1,0:T(8,128)(2,1)} collective-permute-done((bf16[1,128,4096]{2,1,0:T(8,128)(2,1)S(1)}, bf16[1,128,4096]{2,1,0:T(8,128)(2,1)}, u32[]{:S(2)}, u32[]{:S(2)}) %collective-permute-start.12) | collective-permute-done | bytes 1048608 | tf_op jit(solution)/shard_map/ppermute | solution.py:29
  122.2 2.9 %collective-permute-start.17 = (bf16[1,128,4096]{2,1,0:T(8,128)(2,1)S(1)}, bf16[1,128,4096]{2,1,0:T(8,128)(2,1)}, u32[]{:S(2)}, u32[]{:S(2)}) collective-permute-start(bf16[1,128,4096]{2,1,0:T(8,128)(2,1)S(1)} %collective-permute-done.10.refs_6_), channel_id=1, source_target_pairs={{0,12},{1,13},{2,14},{3,15},{4,0},{5,1},{6,2},{7,3},{8,4},{9,5},{1... | collective-permute-start | bytes 3145736 | tf_op jit(solution)/shard_map/ppermute | solution.py:29
  125.1 2.2 %pad_maximum_fusion.2 = bf16[4,896,128]{2,1,0:T(8,128)(2,1)} fusion(bf16[1,896,128]{2,1,0:T(8,128)(2,1)} %get-tuple-element.157, bf16[1,896,128]{2,1,0:T(8,128)(2,1)S(1)} %get-tuple-element.155, bf16[1,896,128]{2,1,0:T(8,128)(2,1)} %get-tuple-element.152, bf16[1,896,128]{2,1,0:T(8,128)(2,1)} %get-tuple-element.149), kind=kLoop, calls=%fused_computation.2 | loop fusion | flops 1376256 | bytes 1835008 | tf_op jit(solution)/shard_map/stack | solution.py:166
  127.3 11.4 %collective-permute-done.14.refs_4_ = bf16[1,128,4096]{2,1,0:T(8,128)(2,1)} collective-permute-done((bf16[1,128,4096]{2,1,0:T(8,128)(2,1)S(1)}, bf16[1,128,4096]{2,1,0:T(8,128)(2,1)}, u32[]{:S(2)}, u32[]{:S(2)}) %collective-permute-start.14) | collective-permute-done | bytes 1048608 | tf_op jit(solution)/shard_map/ppermute | solution.py:29
  138.7 6.0 %collective-permute-done.15.refs_14_ = bf16[1,128,4096]{2,1,0:T(8,128)(2,1)} collective-permute-done((bf16[1,128,4096]{2,1,0:T(8,128)(2,1)}, bf16[1,128,4096]{2,1,0:T(8,128)(2,1)}, u32[]{:S(2)}, u32[]{:S(2)}) %collective-permute-start.15) | collective-permute-done | bytes 1048608 | tf_op jit(solution)/shard_map/ppermute | solution.py:29
  144.7 1.6 collective-permute-start.19
  146.3 1.2 copy-done.3
  147.5 1.2 copy-done.5
  148.6 1.2 copy-done.6
  149.9 12.5 %shard_map.77 = (f32[1,896,4096]{2,1,0:T(8,128)S(1)}, f32[8,128]{1,0:T(8,128)S(1)}) custom-call(bf16[4,896,128]{2,1,0:T(8,128)(2,1)S(1)} %copy-done.3, bf16[4,896,128]{2,1,0:T(8,128)(2,1)} %collective-permute-done.6.refs_1_, bf16[4,896,128]{2,1,0:T(8,128)(2,1)} %collective-permute-done.9.refs_2_, bf16[4,896,128]{2,1,0:T(8,128)(2,1)S(1)} %copy-done.5, ...), custom_call_target="tpu_custom_call" | custom-call | flops 7516192768 | bytes 24903680 | tf_op jit(solution)/shard_map/pallas_call | solution.py:96
  162.3 1.1 collective-permute-done.16.refs_0_.refs_1_.refs_2_
  163.4 1.1 collective-permute-done.17.refs_9_
  164.5 2.9 %collective-permute-start.21 = (bf16[1,128,4096]{2,1,0:T(8,128)(2,1)}, bf16[1,128,4096]{2,1,0:T(8,128)(2,1)S(1)}, u32[]{:S(2)}, u32[]{:S(2)}) collective-permute-start(bf16[1,128,4096]{2,1,0:T(8,128)(2,1)} %collective-permute-done.17.refs_9_), channel_id=1, source_target_pairs={{0,12},{1,13},{2,14},{3,15},{4,0},{5,1},{6,2},{7,3},{8,4},{9,5},{1... | collective-permute-start | bytes 3145736 | tf_op jit(solution)/shard_map/ppermute | solution.py:29
  167.5 8.2 %shard_map.78 = (f32[1,896,4096]{2,1,0:T(8,128)S(1)}, f32[8,128]{1,0:T(8,128)S(1)}) custom-call(bf16[4,896,128]{2,1,0:T(8,128)(2,1)S(1)} %collective-permute-done.16.refs_0_.refs_1_.refs_2_, bf16[4,896,128]{2,1,0:T(8,128)(2,1)S(1)} %collective-permute-done.16.refs_0_.refs_1_.refs_2_, ...), custom_call_target="tpu_custom_call", output_to_operand_aliasing={{0}: (7, {})} | custom-call | flops 2818572288 | bytes 18513920 | tf_op jit(solution)/shard_map/pallas_call | solution.py:96
  175.7 5.6 %collective-permute-done.19.refs_5_ = bf16[1,128,4096]{2,1,0:T(8,128)(2,1)S(1)} collective-permute-done((bf16[1,128,4096]{2,1,0:T(8,128)(2,1)}, bf16[1,128,4096]{2,1,0:T(8,128)(2,1)S(1)}, u32[]{:S(2)}, u32[]{:S(2)}) %collective-permute-start.19) | collective-permute-done | bytes 1048608 | tf_op jit(solution)/shard_map/ppermute | solution.py:29
  181.3 7.5 %collective-permute-done.20.refs_1_.refs_2_.refs_3_.refs_4_ = bf16[4,896,128]{2,1,0:T(8,128)(2,1)S(1)} collective-permute-done((bf16[4,896,128]{2,1,0:T(8,128)(2,1)S(1)}, bf16[4,896,128]{2,1,0:T(8,128)(2,1)S(1)}, u32[]{:S(2)}, u32[]{:S(2)}) %collective-permute-start.20) | collective-permute-done | bytes 917536 | tf_op jit(solution)/shard_map/ppermute | solution.py:29
  188.8 10.7 %shard_map.79 = (bf16[1,896,4096]{2,1,0:T(8,128)(2,1)}, f32[8,128]{1,0:T(8,128)}) custom-call(bf16[4,896,128]{2,1,0:T(8,128)(2,1)S(1)} %collective-permute-done.16.refs_0_.refs_1_.refs_2_, bf16[4,896,128]{2,1,0:T(8,128)(2,1)S(1)} %collective-permute-done.20.refs_1_.refs_2_.refs_3_.refs_4_, ...), custom_call_target="tpu_custom_call" | custom-call | flops 4697620480 | bytes 21069824 | tf_op jit(solution)/shard_map/pallas_call | solution.py:96
  199.5 0.7 copy.11
  (21 shorter events, 0.1 us)
Async XLA Ops:
  0.6 44.0 %copy-start = (f32[1,65536]{1,0:T(1,128)S(1)}, f32[1,65536]{1,0:T(1,128)}, u32[]{:S(2)}) copy-start(f32[1,65536]{1,0:T(1,128)} %param.8) | copy-start | bytes 786436
  0.6 25.3 %collective-permute-start = (bf16[1,128,4096]{2,1,0:T(8,128)(2,1)}, bf16[1,128,4096]{2,1,0:T(8,128)(2,1)}, u32[]{:S(2)}, u32[]{:S(2)}) collective-permute-start(bf16[1,128,4096]{2,1,0:T(8,128)(2,1)} %refs_8_.1), channel_id=1, source_target_pairs={{0,1},{1,2},{2,3},{3,0},{4,5},{5,6},{6,7},{7,4},{8,9},{9,10},{10,1... | collective-permute-start | bytes 3145736 | tf_op jit(solution)/shard_map/ppermute | solution.py:29
  2.6 30.3 %collective-permute-start.1 = (bf16[1,128,4096]{2,1,0:T(8,128)(2,1)}, bf16[1,128,4096]{2,1,0:T(8,128)(2,1)}, u32[]{:S(2)}, u32[]{:S(2)}) collective-permute-start(bf16[1,128,4096]{2,1,0:T(8,128)(2,1)} %refs_8_.1), channel_id=1, source_target_pairs={{0,12},{1,13},{2,14},{3,15},{4,0},{5,1},{6,2},{7,3},{8,4},{9,5},{1... | collective-permute-start | bytes 3145736 | tf_op jit(solution)/shard_map/ppermute | solution.py:29
  5.6 27.2 %collective-permute-start.2 = (bf16[1,128,4096]{2,1,0:T(8,128)(2,1)}, bf16[1,128,4096]{2,1,0:T(8,128)(2,1)}, u32[]{:S(2)}, u32[]{:S(2)}) collective-permute-start(bf16[1,128,4096]{2,1,0:T(8,128)(2,1)} %refs_8_.1), channel_id=1, source_target_pairs={{0,4},{1,5},{2,6},{3,7},{4,8},{5,9},{6,10},{7,11},{8,12},{9,13},{1... | collective-permute-start | bytes 3145736 | tf_op jit(solution)/shard_map/ppermute | solution.py:29
  5.7 2.0 %copy-start.1 = (bf16[1,128,14336]{2,1,0:T(8,128)(2,1)S(1)}, bf16[1,128,14336]{2,1,0:T(8,128)(2,1)}, u32[]{:S(2)}) copy-start(bf16[1,128,14336]{2,1,0:T(8,128)(2,1)} %refs_3_) | copy-start | bytes 11010052
  12.4 109.9 %copy-start.2 = (bf16[4,896,128]{2,1,0:T(8,128)(2,1)}, bf16[4,896,128]{2,1,0:T(8,128)(2,1)S(1)}, u32[]{:S(2)}) copy-start(bf16[4,896,128]{2,1,0:T(8,128)(2,1)S(1)} %get-tuple-element.78.refs_0_) | copy-start | bytes 2752516
  25.9 27.3 %collective-permute-start.3 = (bf16[1,128,4096]{2,1,0:T(8,128)(2,1)}, bf16[1,128,4096]{2,1,0:T(8,128)(2,1)S(1)}, u32[]{:S(2)}, u32[]{:S(2)}) collective-permute-start(bf16[1,128,4096]{2,1,0:T(8,128)(2,1)} %collective-permute-done.refs_12_), channel_id=1, source_target_pairs={{0,1},{1,2},{2,3},{3,0},{4,5},{5,6},{6,7},{7,4},{8,9},{9,10},{10,1... | collective-permute-start | bytes 3145736 | tf_op jit(solution)/shard_map/ppermute | solution.py:29
  29.6 24.8 %collective-permute-start.4 = (bf16[4,896,128]{2,1,0:T(8,128)(2,1)}, bf16[4,896,128]{2,1,0:T(8,128)(2,1)}, u32[]{:S(2)}, u32[]{:S(2)}) collective-permute-start(bf16[4,896,128]{2,1,0:T(8,128)(2,1)} %get-tuple-element.92), channel_id=1, source_target_pairs={{0,4},{1,5},{2,6},{3,7},{4,8},{5,9},{6,10},{7,11},{8,12},{9,13},{1... | collective-permute-start | bytes 2752520 | tf_op jit(solution)/shard_map/ppermute | solution.py:29
  31.2 23.5 %collective-permute-start.5 = (bf16[4,896,128]{2,1,0:T(8,128)(2,1)}, bf16[4,896,128]{2,1,0:T(8,128)(2,1)S(1)}, u32[]{:S(2)}, u32[]{:S(2)}) collective-permute-start(bf16[4,896,128]{2,1,0:T(8,128)(2,1)} %get-tuple-element.94), channel_id=1, source_target_pairs={{0,12},{1,13},{2,14},{3,15},{4,0},{5,1},{6,2},{7,3},{8,4},{9,5},{1... | collective-permute-start | bytes 2752520 | tf_op jit(solution)/shard_map/ppermute | solution.py:29
  32.9 44.4 %collective-permute-start.7 = (bf16[1,128,4096]{2,1,0:T(8,128)(2,1)}, bf16[1,128,4096]{2,1,0:T(8,128)(2,1)}, u32[]{:S(2)}, u32[]{:S(2)}) collective-permute-start(bf16[1,128,4096]{2,1,0:T(8,128)(2,1)} %collective-permute-done.1.refs_11_), channel_id=1, source_target_pairs={{0,12},{1,13},{2,14},{3,15},{4,0},{5,1},{6,2},{7,3},{8,4},{9,5},{1... | collective-permute-start | bytes 3145736 | tf_op jit(solution)/shard_map/ppermute | solution.py:29
  34.7 39.4 %collective-permute-start.6 = (bf16[4,896,128]{2,1,0:T(8,128)(2,1)}, bf16[4,896,128]{2,1,0:T(8,128)(2,1)}, u32[]{:S(2)}, u32[]{:S(2)}) collective-permute-start(bf16[4,896,128]{2,1,0:T(8,128)(2,1)} %get-tuple-element.97), channel_id=1, source_target_pairs={{0,4},{1,5},{2,6},{3,7},{4,8},{5,9},{6,10},{7,11},{8,12},{9,13},{1... | collective-permute-start | bytes 2752520 | tf_op jit(solution)/shard_map/ppermute | solution.py:29
  34.9 27.2 %all-to-all-start = ((f32[16,32,128]{2,1,0:T(8,128)}), f32[16,32,128]{2,1,0:T(8,128)S(1)}, u32[]{:S(2)}, u32[]{:S(2)}) async-start(f32[16,32,128]{2,1,0:T(8,128)} %bitcast.20), calls=%async_computation | async-start | bytes 524288 | tf_op jit(solution)/shard_map/all_to_all | solution.py:120
  54.7 1.6 copy-start.4
  54.7 39.1 %collective-permute-start.9 = (bf16[4,896,128]{2,1,0:T(8,128)(2,1)}, bf16[4,896,128]{2,1,0:T(8,128)(2,1)}, u32[]{:S(2)}, u32[]{:S(2)}) collective-permute-start(bf16[4,896,128]{2,1,0:T(8,128)(2,1)} %collective-permute-done.4), channel_id=1, source_target_pairs={{0,4},{1,5},{2,6},{3,7},{4,8},{5,9},{6,10},{7,11},{8,12},{9,13},{1... | collective-permute-start | bytes 2752520 | tf_op jit(solution)/shard_map/ppermute | solution.py:29
  56.3 43.5 %collective-permute-start.8 = (bf16[1,128,4096]{2,1,0:T(8,128)(2,1)}, bf16[1,128,4096]{2,1,0:T(8,128)(2,1)}, u32[]{:S(2)}, u32[]{:S(2)}) collective-permute-start(bf16[1,128,4096]{2,1,0:T(8,128)(2,1)} %collective-permute-done.refs_12_), channel_id=1, source_target_pairs={{0,12},{1,13},{2,14},{3,15},{4,0},{5,1},{6,2},{7,3},{8,4},{9,5},{1... | collective-permute-start | bytes 3145736 | tf_op jit(solution)/shard_map/ppermute | solution.py:29
  58.5 41.2 %collective-permute-start.10 = (bf16[1,128,4096]{2,1,0:T(8,128)(2,1)S(1)}, bf16[1,128,4096]{2,1,0:T(8,128)(2,1)S(1)}, u32[]{:S(2)}, u32[]{:S(2)}) collective-permute-start(bf16[1,128,4096]{2,1,0:T(8,128)(2,1)S(1)} %collective-permute-done.3.refs_3_), channel_id=1, source_target_pairs={{0,1},{1,2},{2,3},{3,0},{4,5},{5,6},{6,7},{7,4},{8,9},{9,10},{10,1... | collective-permute-start | bytes 3145736 | tf_op jit(solution)/shard_map/ppermute | solution.py:29
  77.3 41.5 %collective-permute-start.11 = (bf16[1,128,4096]{2,1,0:T(8,128)(2,1)}, bf16[1,128,4096]{2,1,0:T(8,128)(2,1)}, u32[]{:S(2)}, u32[]{:S(2)}) collective-permute-start(bf16[1,128,4096]{2,1,0:T(8,128)(2,1)} %collective-permute-done.refs_12_), channel_id=1, source_target_pairs={{0,4},{1,5},{2,6},{3,7},{4,8},{5,9},{6,10},{7,11},{8,12},{9,13},{1... | collective-permute-start | bytes 3145736 | tf_op jit(solution)/shard_map/ppermute | solution.py:29
  79.0 43.3 %collective-permute-start.12 = (bf16[1,128,4096]{2,1,0:T(8,128)(2,1)S(1)}, bf16[1,128,4096]{2,1,0:T(8,128)(2,1)}, u32[]{:S(2)}, u32[]{:S(2)}) collective-permute-start(bf16[1,128,4096]{2,1,0:T(8,128)(2,1)S(1)} %collective-permute-done.3.refs_3_), channel_id=1, source_target_pairs={{0,12},{1,13},{2,14},{3,15},{4,0},{5,1},{6,2},{7,3},{8,4},{9,5},{1... | collective-permute-start | bytes 3145736 | tf_op jit(solution)/shard_map/ppermute | solution.py:29
  99.8 22.5 %collective-permute-start.13 = (bf16[4,896,128]{2,1,0:T(8,128)(2,1)}, bf16[4,896,128]{2,1,0:T(8,128)(2,1)}, u32[]{:S(2)}, u32[]{:S(2)}) collective-permute-start(bf16[4,896,128]{2,1,0:T(8,128)(2,1)} %pad_maximum_fusion), channel_id=1, source_target_pairs={{0,1},{1,2},{2,3},{3,0},{4,5},{5,6},{6,7},{7,4},{8,9},{9,10},{10,1... | collective-permute-start | bytes 2752520 | tf_op jit(solution)/shard_map/ppermute | solution.py:29
  99.8 38.9 %collective-permute-start.14 = (bf16[1,128,4096]{2,1,0:T(8,128)(2,1)S(1)}, bf16[1,128,4096]{2,1,0:T(8,128)(2,1)}, u32[]{:S(2)}, u32[]{:S(2)}) collective-permute-start(bf16[1,128,4096]{2,1,0:T(8,128)(2,1)S(1)} %collective-permute-done.3.refs_3_), channel_id=1, source_target_pairs={{0,4},{1,5},{2,6},{3,7},{4,8},{5,9},{6,10},{7,11},{8,12},{9,13},{1... | collective-permute-start | bytes 3145736 | tf_op jit(solution)/shard_map/ppermute | solution.py:29
  101.3 43.4 %collective-permute-start.15 = (bf16[1,128,4096]{2,1,0:T(8,128)(2,1)}, bf16[1,128,4096]{2,1,0:T(8,128)(2,1)}, u32[]{:S(2)}, u32[]{:S(2)}) collective-permute-start(bf16[1,128,4096]{2,1,0:T(8,128)(2,1)} %collective-permute-done.8.refs_15_), channel_id=1, source_target_pairs={{0,12},{1,13},{2,14},{3,15},{4,0},{5,1},{6,2},{7,3},{8,4},{9,5},{1... | collective-permute-start | bytes 3145736 | tf_op jit(solution)/shard_map/ppermute | solution.py:29
  105.8 21.5 %all-to-all-start.1 = ((f32[16,32,128]{2,1,0:T(8,128)}), f32[16,32,128]{2,1,0:T(8,128)S(1)}, u32[]{:S(2)}, u32[]{:S(2)}) async-start(f32[16,32,128]{2,1,0:T(8,128)} %broadcast_in_dim.13), calls=%async_computation.1 | async-start | bytes 524288 | tf_op jit(solution)/shard_map/all_to_all | solution.py:134
  122.2 42.3 %collective-permute-start.17 = (bf16[1,128,4096]{2,1,0:T(8,128)(2,1)S(1)}, bf16[1,128,4096]{2,1,0:T(8,128)(2,1)}, u32[]{:S(2)}, u32[]{:S(2)}) collective-permute-start(bf16[1,128,4096]{2,1,0:T(8,128)(2,1)S(1)} %collective-permute-done.10.refs_6_), channel_id=1, source_target_pairs={{0,12},{1,13},{2,14},{3,15},{4,0},{5,1},{6,2},{7,3},{8,4},{9,5},{1... | collective-permute-start | bytes 3145736 | tf_op jit(solution)/shard_map/ppermute | solution.py:29
  125.1 38.3 %collective-permute-start.16 = (bf16[4,896,128]{2,1,0:T(8,128)(2,1)}, bf16[4,896,128]{2,1,0:T(8,128)(2,1)S(1)}, u32[]{:S(2)}, u32[]{:S(2)}) collective-permute-start(bf16[4,896,128]{2,1,0:T(8,128)(2,1)} %pad_maximum_fusion.1), channel_id=1, source_target_pairs={{0,2},{1,3},{2,0},{3,1},{4,6},{5,7},{6,4},{7,5},{8,10},{9,11},{10,... | collective-permute-start | bytes 2752520 | tf_op jit(solution)/shard_map/ppermute | solution.py:29
  127.3 48.4 %collective-permute-start.18 = (bf16[1,128,4096]{2,1,0:T(8,128)(2,1)S(1)}, bf16[1,128,4096]{2,1,0:T(8,128)(2,1)}, u32[]{:S(2)}, u32[]{:S(2)}) collective-permute-start(bf16[1,128,4096]{2,1,0:T(8,128)(2,1)S(1)} %collective-permute-done.10.refs_6_), channel_id=1, source_target_pairs={{0,4},{1,5},{2,6},{3,7},{4,8},{5,9},{6,10},{7,11},{8,12},{9,13},{1... | collective-permute-start | bytes 3145736 | tf_op jit(solution)/shard_map/ppermute | solution.py:29
  144.7 36.6 %collective-permute-start.19 = (bf16[1,128,4096]{2,1,0:T(8,128)(2,1)}, bf16[1,128,4096]{2,1,0:T(8,128)(2,1)S(1)}, u32[]{:S(2)}, u32[]{:S(2)}) collective-permute-start(bf16[1,128,4096]{2,1,0:T(8,128)(2,1)} %collective-permute-done.14.refs_4_), channel_id=1, source_target_pairs={{0,4},{1,5},{2,6},{3,7},{4,8},{5,9},{6,10},{7,11},{8,12},{9,13},{1... | collective-permute-start | bytes 3145736 | tf_op jit(solution)/shard_map/ppermute | solution.py:29
  146.3 1.2 copy-start.3
  147.5 1.2 copy-start.5
  148.6 1.2 copy-start.6
  149.9 17.6 %copy-start.7 = (bf16[4,896,128]{2,1,0:T(8,128)(2,1)S(1)}, bf16[4,896,128]{2,1,0:T(8,128)(2,1)}, u32[]{:S(2)}) copy-start(bf16[4,896,128]{2,1,0:T(8,128)(2,1)} %pad_maximum_fusion.2) | copy-start | bytes 2752516
  164.5 24.3 %collective-permute-start.21 = (bf16[1,128,4096]{2,1,0:T(8,128)(2,1)}, bf16[1,128,4096]{2,1,0:T(8,128)(2,1)S(1)}, u32[]{:S(2)}, u32[]{:S(2)}) collective-permute-start(bf16[1,128,4096]{2,1,0:T(8,128)(2,1)} %collective-permute-done.17.refs_9_), channel_id=1, source_target_pairs={{0,12},{1,13},{2,14},{3,15},{4,0},{5,1},{6,2},{7,3},{8,4},{9,5},{1... | collective-permute-start | bytes 3145736 | tf_op jit(solution)/shard_map/ppermute | solution.py:29
  167.5 21.3 %collective-permute-start.20 = (bf16[4,896,128]{2,1,0:T(8,128)(2,1)S(1)}, bf16[4,896,128]{2,1,0:T(8,128)(2,1)S(1)}, u32[]{:S(2)}, u32[]{:S(2)}) collective-permute-start(bf16[4,896,128]{2,1,0:T(8,128)(2,1)S(1)} %copy-done.7), channel_id=1, source_target_pairs={{0,3},{1,0},{2,1},{3,2},{4,7},{5,4},{6,5},{7,6},{8,11},{9,8},{10,9... | collective-permute-start | bytes 2752520 | tf_op jit(solution)/shard_map/ppermute | solution.py:29

commit v2 on v1

--- a/solution.py
+++ b/solution.py
@@ -162,16 +162,23 @@
     def along(k):
         return (f"b{k}", lambda: env[f"b{k - 1}"], 0, 1)
 
-    def spread(s):
-        return (f"X{s}", lambda: jnp.stack([env[f"R{d}"][s] for d in every]), 0, s)
+    def spread(s, near=range(NY), name=""):
+        def packed():
+            return jnp.stack([env[f"R{d}"][s] for d in near])
+
+        for i, d in enumerate(near):
+            where[s, d] = (f"X{s}{name}", i)
+        return (f"X{s}{name}", packed, 0, s)
+
+    where = {(0, d): (f"R{d}", 0) for d in range(NY)}
 
     def compute(name, pairs, total=None, final=False):
         blocks = []
         for k, d in pairs:
-            array, row = (env[f"R{d}"], 0) if k == 0 else (env[f"X{k}"], d)
-            names = [("b", "p", "f", "m")[d] + str(k)]
-            right = [env[part] for part in names]
-            blocks.append((array, row, right))
+            array, row = where[k, d]
+            part = ("b", "p", "f", "m")[d] + str(k)
+            right = [env[part]] if part in env else [env[part + "y"], env[part + "z"]]
+            blocks.append((env[array], row, right))
         env[name], env["token"] = matmul(blocks, env["token"], total, final)
 
     every = range(NY)
@@ -189,17 +196,21 @@
     event(["q2", "R3"], [("R2", lambda: env["q2"], 1, 0), down(1)])
     event(["R1", "f0", "shares"], [up(1), down(2)])
     moment, updated = outer_update(env["shares"], outer_params, momentum)
-    event(["R2", "m1", "b3"], [up(2), far(1, -1), spread(1)])
+    event(["R2"], [spread(1), up(2)])
+    event(["m1", "b3"], [far(1, -1)])
     env["params"] = hand_out(*past(updated))
     event(["p1", "m2", "X1"], [up(3), down(3), spread(2)])
     event(["p2", "f1", "params"], [far(2, 1)])
+    env["params"] = env["params"].reshape(1, -1)
     compute("t1", [(k, d) for k in (0, 1) for d in every])
+    event(["m3"], [far(3, -1)])
     event(["X2"], [spread(3)])
-    event(["m3"], [far(3, -1)])
     compute("t2", [(2, d) for d in (0, 1, 3)], env["t1"])
-    event(["p3", "f2", "X3", "f3"], [])
-    compute("out", [(2, 2), (3, 0), (3, 1), (3, 2), (3, 3)], env["t2"], final=True)
-    return env["out"], moment[None], env["params"].reshape(1, -1)
+    event(["f2", "p3"], [])
+    compute("t3", [(2, 2)], env["t2"])
+    event(["X3", "f3", "params"], [])
+    compute("out", [(3, 0), (3, 1), (3, 2), (3, 3)], env["t3"], final=True)
+    return env["out"], moment[None], env["params"]
 
 
 def solution(mesh):

time: 204 us -> 200 us (0.980); the launches traced: 200 us -> 199 us
  Pallas kernels: 36 us -> 40 us
  waiting for transfers between devices: 86.6 us -> 82.9 us
  other arithmetic: 8.6 us -> 6.49 us
    pallas_call x3 -> x4, Pallas kernels: 31.4 us -> 35.4 us  [matmul(): pl.pallas_call(kernel, grid=(COLUMNS // width,), in_specs=in_specs, out_s...]
    ppermute x22, waiting for transfers between devices: 86.6 us -> 82.9 us  [fsdp_send(): return lax.ppermute(array, 'fsdp', shift(dy, dz))]
    another operation x3, other arithmetic: 6.42 us -> 4.31 us  [packed(): return jnp.stack([env[f'R{d}'][s] for d in near])]
    unnamed x17 -> x23, local copies, waits for them, and re-layouts: 6.34 us -> 6.35 us
  transfers between devices with their start and end apart: 24 -> 24, of which waited for: 15 -> 15; matrix products, arithmetic and copies ran while one was open for 8% -> 8% of each run, Pallas kernels for 13% -> 15%
where the time goes in v2:
time: 200 us; the launch traced here: 199 us
  waiting for transfers between devices  82.9 us (41%)
  starting transfers between devices  53.8 us (27%)
  Pallas kernels  40 us (20%)
  local copies, waits for them, and re-layouts  15.2 us (8%)
  other arithmetic  6.49 us (3%)
    ppermute x22, waiting for transfers between devices, fsdp_send(): return lax.ppermute(array, 'fsdp', shift(dy, dz))  82.9 us
    pallas_call x4, Pallas kernels, matmul(): pl.pallas_call(kernel, grid=(COLUMNS // width,), in_specs=in_specs, out_s...  35.4 us
    ppermute x22, starting transfers between devices, fsdp_send(): return lax.ppermute(array, 'fsdp', shift(dy, dz))  34.5 us
    all_to_all x1, starting transfers between devices, hand_out(): return lax.all_to_all(copies, 'replica', 0, 0, tiled=True)  9.68 us
    all_to_all x1, starting transfers between devices, reduce_shares(): return lax.all_to_all(pieces, 'replica', 0, 0, tiled=True)  9.68 us
    slice x5, local copies, waits for them, and re-layouts, packed(): return jnp.stack([env[f'R{d}'][s] for d in near])  7.52 us
    unnamed x23, local copies, waits for them, and re-layouts  6.35 us
    pallas_call x1, Pallas kernels, activate(): pl.pallas_call(activate_kernel, grid_spec=pltpu.PrefetchScalarGridSpec(nu...  4.62 us
  transfers between devices with their start and end apart: 24, of which 15 were waited for; matrix products, arithmetic and copies ran while one was open for 8% of the time, Pallas kernels for 15%

profile of v2, /device:TPU:224, one launch (start us, length us, event | category | flops | bytes accessed | tf_op | source)
XLA Modules:
  0.0 199.2 jit_solution(15712150483134113714)
XLA Ops:
  0.6 0.0 copy-start
  0.6 2.0 collective-permute-start
  2.6 3.0 %collective-permute-start.1 = (bf16[1,128,4096]{2,1,0:T(8,128)(2,1)}, bf16[1,128,4096]{2,1,0:T(8,128)(2,1)}, u32[]{:S(2)}, u32[]{:S(2)}) collective-permute-start(bf16[1,128,4096]{2,1,0:T(8,128)(2,1)} %refs_8_.1), channel_id=1, source_target_pairs={{0,12},{1,13},{2,14},{3,15},{4,0},{5,1},{6,2},{7,3},{8,4},{9,5},{1... | collective-permute-start | bytes 3145736 | tf_op jit(solution)/shard_map/ppermute | solution.py:29
  5.6 0.0 collective-permute-start.2
  5.6 0.1 pad_add_fusion.place_ref
  5.7 2.0 %copy-done.1 = bf16[1,128,14336]{2,1,0:T(8,128)(2,1)S(1)} copy-done((bf16[1,128,14336]{2,1,0:T(8,128)(2,1)S(1)}, bf16[1,128,14336]{2,1,0:T(8,128)(2,1)}, u32[]{:S(2)}) %copy-start.1) | copy-done | bytes 3670040
  7.8 4.6 %shard_map.76 = (bf16[4,896,128]{2,1,0:T(8,128)(2,1)S(1)}, bf16[4,896,128]{2,1,0:T(8,128)(2,1)}, bf16[4,896,128]{2,1,0:T(8,128)(2,1)}, bf16[4,896,128]{2,1,0:T(8,128)(2,1)}) custom-call(s32[2]{0:T(128)S(1)} %pad_add_fusion.place_ref, bf16[1,128,14336]{2,1,0:T(8,128)(2,1)S(1)} %copy-done.1, bf16[1,128,14336]{2,1,0:T(8,128)(2,1)S(1)} %copy-done.1, ...), custom_call_target="tpu_custom_call" | custom-call | tf_op jit(solution)/shard_map/pallas_call | solution.py:43
  12.4 13.6 %collective-permute-done.refs_12_ = bf16[1,128,4096]{2,1,0:T(8,128)(2,1)} collective-permute-done((bf16[1,128,4096]{2,1,0:T(8,128)(2,1)}, bf16[1,128,4096]{2,1,0:T(8,128)(2,1)}, u32[]{:S(2)}, u32[]{:S(2)}) %collective-permute-start) | collective-permute-done | bytes 1048608 | tf_op jit(solution)/shard_map/ppermute | solution.py:29
  25.9 3.7 %collective-permute-start.3 = (bf16[1,128,4096]{2,1,0:T(8,128)(2,1)}, bf16[1,128,4096]{2,1,0:T(8,128)(2,1)S(1)}, u32[]{:S(2)}, u32[]{:S(2)}) collective-permute-start(bf16[1,128,4096]{2,1,0:T(8,128)(2,1)} %collective-permute-done.refs_12_), channel_id=1, source_target_pairs={{0,1},{1,2},{2,3},{3,0},{4,5},{5,6},{6,7},{7,4},{8,9},{9,10},{10,1... | collective-permute-start | bytes 3145736 | tf_op jit(solution)/shard_map/ppermute | solution.py:29
  29.6 1.6 collective-permute-start.4
  31.2 1.7 collective-permute-start.5
  32.9 1.8 collective-permute-start.7
  34.7 0.2 collective-permute-start.6
  34.9 9.7 %all-to-all-start = ((f32[16,32,128]{2,1,0:T(8,128)}), f32[16,32,128]{2,1,0:T(8,128)S(1)}, u32[]{:S(2)}, u32[]{:S(2)}) async-start(f32[16,32,128]{2,1,0:T(8,128)} %bitcast.20), calls=%async_computation | async-start | bytes 524288 | tf_op jit(solution)/shard_map/all_to_all | solution.py:120
  44.6 0.6 constant_dynamic-slice_fusion
  45.2 8.0 %collective-permute-done.3.refs_3_ = bf16[1,128,4096]{2,1,0:T(8,128)(2,1)S(1)} collective-permute-done((bf16[1,128,4096]{2,1,0:T(8,128)(2,1)}, bf16[1,128,4096]{2,1,0:T(8,128)(2,1)S(1)}, u32[]{:S(2)}, u32[]{:S(2)}) %collective-permute-start.3) | collective-permute-done | bytes 1048608 | tf_op jit(solution)/shard_map/ppermute | solution.py:29
  53.2 1.2 collective-permute-done.4
  54.4 0.3 collective-permute-done.5.refs_3_
  54.7 1.6 collective-permute-start.8
  56.3 2.2 %collective-permute-start.9 = (bf16[1,128,4096]{2,1,0:T(8,128)(2,1)}, bf16[1,128,4096]{2,1,0:T(8,128)(2,1)}, u32[]{:S(2)}, u32[]{:S(2)}) collective-permute-start(bf16[1,128,4096]{2,1,0:T(8,128)(2,1)} %collective-permute-done.refs_12_), channel_id=1, source_target_pairs={{0,12},{1,13},{2,14},{3,15},{4,0},{5,1},{6,2},{7,3},{8,4},{9,5},{1... | collective-permute-start | bytes 3145736 | tf_op jit(solution)/shard_map/ppermute | solution.py:29
  58.5 2.7 %collective-permute-start.10 = (bf16[1,128,4096]{2,1,0:T(8,128)(2,1)S(1)}, bf16[1,128,4096]{2,1,0:T(8,128)(2,1)S(1)}, u32[]{:S(2)}, u32[]{:S(2)}) collective-permute-start(bf16[1,128,4096]{2,1,0:T(8,128)(2,1)S(1)} %collective-permute-done.3.refs_3_), channel_id=1, source_target_pairs={{0,1},{1,2},{2,3},{3,0},{4,5},{5,6},{6,7},{7,4},{8,9},{9,10},{10,1... | collective-permute-start | bytes 3145736 | tf_op jit(solution)/shard_map/ppermute | solution.py:29
  61.2 0.9 fusion.4
  62.1 0.0 all-to-all-done
  62.1 12.0 %collective-permute-done.6.refs_1_ = bf16[4,896,128]{2,1,0:T(8,128)(2,1)} collective-permute-done((bf16[4,896,128]{2,1,0:T(8,128)(2,1)}, bf16[4,896,128]{2,1,0:T(8,128)(2,1)}, u32[]{:S(2)}, u32[]{:S(2)}) %collective-permute-start.6) | collective-permute-done | bytes 917536 | tf_op jit(solution)/shard_map/ppermute | solution.py:29
  74.1 3.2 %collective-permute-done.7.refs_10_ = bf16[1,128,4096]{2,1,0:T(8,128)(2,1)} collective-permute-done((bf16[1,128,4096]{2,1,0:T(8,128)(2,1)}, bf16[1,128,4096]{2,1,0:T(8,128)(2,1)}, u32[]{:S(2)}, u32[]{:S(2)}) %collective-permute-start.7) | collective-permute-done | bytes 1048608 | tf_op jit(solution)/shard_map/ppermute | solution.py:29
  77.3 1.7 collective-permute-start.11
  79.0 1.7 collective-permute-start.12
  80.6 2.0 fusion.5
  82.6 2.0 fusion.7
  84.6 9.2 %collective-permute-done.8.refs_2_ = bf16[4,896,128]{2,1,0:T(8,128)(2,1)} collective-permute-done((bf16[4,896,128]{2,1,0:T(8,128)(2,1)}, bf16[4,896,128]{2,1,0:T(8,128)(2,1)}, u32[]{:S(2)}, u32[]{:S(2)}) %collective-permute-start.8) | collective-permute-done | bytes 917536 | tf_op jit(solution)/shard_map/ppermute | solution.py:29
  93.8 1.0 slice.48
  94.7 2.0 %pad_maximum_fusion = bf16[4,896,128]{2,1,0:T(8,128)(2,1)} fusion(bf16[1,896,128]{2,1,0:T(8,128)(2,1)S(1)} %get-tuple-element.169, bf16[1,896,128]{2,1,0:T(8,128)(2,1)S(1)} %slice.48, bf16[1,896,128]{2,1,0:T(8,128)(2,1)S(1)} %get-tuple-element.164, bf16[1,896,128]{2,1,0:T(8,128)(2,1)} %get-tuple-element.161), kind=kLoop, calls=%fused_computation | loop fusion | flops 1376256 | bytes 1835008 | tf_op jit(solution)/shard_map/stack | solution.py:167
  96.7 0.0 collective-permute-start.13
  96.7 3.0 %collective-permute-done.9.refs_15_ = bf16[1,128,4096]{2,1,0:T(8,128)(2,1)} collective-permute-done((bf16[1,128,4096]{2,1,0:T(8,128)(2,1)}, bf16[1,128,4096]{2,1,0:T(8,128)(2,1)}, u32[]{:S(2)}, u32[]{:S(2)}) %collective-permute-start.9) | collective-permute-done | bytes 1048608 | tf_op jit(solution)/shard_map/ppermute | solution.py:29
  99.8 1.6 collective-permute-start.14
  101.3 1.7 collective-permute-start.15
  103.0 1.4 fusion.3
  104.3 0.7 fusion.2
  105.1 0.7 broadcast_in_dim.13
  105.8 9.7 %all-to-all-start.1 = ((f32[16,32,128]{2,1,0:T(8,128)}), f32[16,32,128]{2,1,0:T(8,128)S(1)}, u32[]{:S(2)}, u32[]{:S(2)}) async-start(f32[16,32,128]{2,1,0:T(8,128)} %broadcast_in_dim.13), calls=%async_computation.1 | async-start | bytes 524288 | tf_op jit(solution)/shard_map/all_to_all | solution.py:134
  115.5 1.8 fusion.6
  117.3 2.2 %pad_maximum_fusion.1 = bf16[4,896,128]{2,1,0:T(8,128)(2,1)} fusion(bf16[1,896,128]{2,1,0:T(8,128)(2,1)} %get-tuple-element.168, bf16[1,896,128]{2,1,0:T(8,128)(2,1)S(1)} %get-tuple-element.166, bf16[1,896,128]{2,1,0:T(8,128)(2,1)} %get-tuple-element.163, bf16[1,896,128]{2,1,0:T(8,128)(2,1)} %get-tuple-element.160), kind=kLoop, calls=%fused_computation.1 | loop fusion | flops 1376256 | bytes 1835008 | tf_op jit(solution)/shard_map/stack | solution.py:167
  119.5 0.0 collective-permute-done.11.refs_13_
  119.5 2.8 %collective-permute-done.12.refs_5_ = bf16[1,128,4096]{2,1,0:T(8,128)(2,1)} collective-permute-done((bf16[1,128,4096]{2,1,0:T(8,128)(2,1)S(1)}, bf16[1,128,4096]{2,1,0:T(8,128)(2,1)}, u32[]{:S(2)}, u32[]{:S(2)}) %collective-permute-start.12) | collective-permute-done | bytes 1048608 | tf_op jit(solution)/shard_map/ppermute | solution.py:29
  122.2 0.0 collective-permute-done.13.refs_4_.refs_5_.refs_6_.refs_7_
  122.2 2.9 %collective-permute-start.16 = (bf16[1,128,4096]{2,1,0:T(8,128)(2,1)S(1)}, bf16[1,128,4096]{2,1,0:T(8,128)(2,1)}, u32[]{:S(2)}, u32[]{:S(2)}) collective-permute-start(bf16[1,128,4096]{2,1,0:T(8,128)(2,1)S(1)} %collective-permute-done.10.refs_4_), channel_id=1, source_target_pairs={{0,12},{1,13},{2,14},{3,15},{4,0},{5,1},{6,2},{7,3},{8,4},{9,5},{1... | collective-permute-start | bytes 3145736 | tf_op jit(solution)/shard_map/ppermute | solution.py:29
  125.1 0.1 all-to-all-done.1
  125.2 13.5 %collective-permute-done.14.refs_4_ = bf16[1,128,4096]{2,1,0:T(8,128)(2,1)} collective-permute-done((bf16[1,128,4096]{2,1,0:T(8,128)(2,1)S(1)}, bf16[1,128,4096]{2,1,0:T(8,128)(2,1)}, u32[]{:S(2)}, u32[]{:S(2)}) %collective-permute-start.14) | collective-permute-done | bytes 1048608 | tf_op jit(solution)/shard_map/ppermute | solution.py:29
  138.7 6.0 %collective-permute-done.15.refs_14_ = bf16[1,128,4096]{2,1,0:T(8,128)(2,1)} collective-permute-done((bf16[1,128,4096]{2,1,0:T(8,128)(2,1)}, bf16[1,128,4096]{2,1,0:T(8,128)(2,1)}, u32[]{:S(2)}, u32[]{:S(2)}) %collective-permute-start.15) | collective-permute-done | bytes 1048608 | tf_op jit(solution)/shard_map/ppermute | solution.py:29
  144.7 1.6 collective-permute-start.18
  146.3 1.2 copy-done.3
  147.5 1.2 copy-done.5
  148.6 1.2 copy-done.6
  149.9 12.5 %shard_map.77 = (f32[1,896,4096]{2,1,0:T(8,128)S(1)}, f32[8,128]{1,0:T(8,128)S(1)}) custom-call(bf16[4,896,128]{2,1,0:T(8,128)(2,1)S(1)} %copy-done.3, bf16[4,896,128]{2,1,0:T(8,128)(2,1)} %collective-permute-done.6.refs_1_, bf16[4,896,128]{2,1,0:T(8,128)(2,1)} %collective-permute-done.8.refs_2_, bf16[4,896,128]{2,1,0:T(8,128)(2,1)S(1)} %copy-done.5, ...), custom_call_target="tpu_custom_call" | custom-call | flops 7516192768 | bytes 24903680 | tf_op jit(solution)/shard_map/pallas_call | solution.py:96
  162.4 2.2 %collective-permute-done.16.refs_7_ = bf16[1,128,4096]{2,1,0:T(8,128)(2,1)} collective-permute-done((bf16[1,128,4096]{2,1,0:T(8,128)(2,1)S(1)}, bf16[1,128,4096]{2,1,0:T(8,128)(2,1)}, u32[]{:S(2)}, u32[]{:S(2)}) %collective-permute-start.16) | collective-permute-done | bytes 1048608 | tf_op jit(solution)/shard_map/ppermute | solution.py:29
  164.5 2.9 %collective-permute-start.21 = (bf16[1,128,4096]{2,1,0:T(8,128)(2,1)}, bf16[1,128,4096]{2,1,0:T(8,128)(2,1)S(1)}, u32[]{:S(2)}, u32[]{:S(2)}) collective-permute-start(bf16[1,128,4096]{2,1,0:T(8,128)(2,1)} %collective-permute-done.16.refs_7_), channel_id=1, source_target_pairs={{0,12},{1,13},{2,14},{3,15},{4,0},{5,1},{6,2},{7,3},{8,4},{9,5},{1... | collective-permute-start | bytes 3145736 | tf_op jit(solution)/shard_map/ppermute | solution.py:29
  167.5 0.1 pad_maximum_fusion.2
  167.6 0.1 collective-permute-start.20
  167.7 8.2 %shard_map.78 = (f32[1,896,4096]{2,1,0:T(8,128)S(1)}, f32[8,128]{1,0:T(8,128)S(1)}) custom-call(bf16[4,896,128]{2,1,0:T(8,128)(2,1)S(1)} %collective-permute-done.17.refs_0_.refs_1_.refs_2_, bf16[4,896,128]{2,1,0:T(8,128)(2,1)S(1)} %collective-permute-done.17.refs_0_.refs_1_.refs_2_, ...), custom_call_target="tpu_custom_call", output_to_operand_aliasing={{0}: (7, {})} | custom-call | flops 2818572288 | bytes 18513920 | tf_op jit(solution)/shard_map/pallas_call | solution.py:96
  175.9 5.3 %collective-permute-done.18.refs_1_ = bf16[1,128,4096]{2,1,0:T(8,128)(2,1)S(1)} collective-permute-done((bf16[1,128,4096]{2,1,0:T(8,128)(2,1)}, bf16[1,128,4096]{2,1,0:T(8,128)(2,1)S(1)}, u32[]{:S(2)}, u32[]{:S(2)}) %collective-permute-start.18) | collective-permute-done | bytes 1048608 | tf_op jit(solution)/shard_map/ppermute | solution.py:29
  181.3 5.2 %shard_map.79 = (f32[1,896,4096]{2,1,0:T(8,128)S(1)}, f32[8,128]{1,0:T(8,128)S(1)}) custom-call(bf16[4,896,128]{2,1,0:T(8,128)(2,1)S(1)} %collective-permute-done.17.refs_0_.refs_1_.refs_2_, bf16[1,128,4096]{2,1,0:T(8,128)(2,1)S(1)} %collective-permute-done.18.refs_1_, f32[8,128]{1,0:T(8,128)S(1)} %get-tuple-element.145.refs_2_, ...), custom_call_target="tpu_custom_call", output_to_operand_aliasing={{0}: (3, {})} | custom-call | flops 939524096 | bytes 15958016 | tf_op jit(solution)/shard_map/pallas_call | solution.py:96
  186.4 2.6 %collective-permute-done.20.refs_0_.refs_1_.refs_2_.refs_3_ = bf16[4,896,128]{2,1,0:T(8,128)(2,1)S(1)} collective-permute-done((bf16[4,896,128]{2,1,0:T(8,128)(2,1)S(1)}, bf16[4,896,128]{2,1,0:T(8,128)(2,1)S(1)}, u32[]{:S(2)}, u32[]{:S(2)}) %collective-permute-start.20) | collective-permute-done | bytes 917536 | tf_op jit(solution)/shard_map/ppermute | solution.py:29
  189.0 9.5 %shard_map.80 = (bf16[1,896,4096]{2,1,0:T(8,128)(2,1)}, f32[8,128]{1,0:T(8,128)}) custom-call(bf16[4,896,128]{2,1,0:T(8,128)(2,1)S(1)} %collective-permute-done.20.refs_0_.refs_1_.refs_2_.refs_3_, bf16[4,896,128]{2,1,0:T(8,128)(2,1)S(1)} %collective-permute-done.20.refs_0_.refs_1_.refs_2_.refs_3_, ...), custom_call_target="tpu_custom_call" | custom-call | flops 3758096384 | bytes 19791872 | tf_op jit(solution)/shard_map/pallas_call | solution.py:96
  198.5 0.7 copy.13
  (28 shorter events, 0.1 us)
Async XLA Ops:
  0.6 44.0 %copy-start = (f32[1,65536]{1,0:T(1,128)S(1)}, f32[1,65536]{1,0:T(1,128)}, u32[]{:S(2)}) copy-start(f32[1,65536]{1,0:T(1,128)} %param.8) | copy-start | bytes 786436
  0.6 25.3 %collective-permute-start = (bf16[1,128,4096]{2,1,0:T(8,128)(2,1)}, bf16[1,128,4096]{2,1,0:T(8,128)(2,1)}, u32[]{:S(2)}, u32[]{:S(2)}) collective-permute-start(bf16[1,128,4096]{2,1,0:T(8,128)(2,1)} %refs_8_.1), channel_id=1, source_target_pairs={{0,1},{1,2},{2,3},{3,0},{4,5},{5,6},{6,7},{7,4},{8,9},{9,10},{10,1... | collective-permute-start | bytes 3145736 | tf_op jit(solution)/shard_map/ppermute | solution.py:29
  2.6 30.3 %collective-permute-start.1 = (bf16[1,128,4096]{2,1,0:T(8,128)(2,1)}, bf16[1,128,4096]{2,1,0:T(8,128)(2,1)}, u32[]{:S(2)}, u32[]{:S(2)}) collective-permute-start(bf16[1,128,4096]{2,1,0:T(8,128)(2,1)} %refs_8_.1), channel_id=1, source_target_pairs={{0,12},{1,13},{2,14},{3,15},{4,0},{5,1},{6,2},{7,3},{8,4},{9,5},{1... | collective-permute-start | bytes 3145736 | tf_op jit(solution)/shard_map/ppermute | solution.py:29
  5.6 27.2 %collective-permute-start.2 = (bf16[1,128,4096]{2,1,0:T(8,128)(2,1)}, bf16[1,128,4096]{2,1,0:T(8,128)(2,1)}, u32[]{:S(2)}, u32[]{:S(2)}) collective-permute-start(bf16[1,128,4096]{2,1,0:T(8,128)(2,1)} %refs_8_.1), channel_id=1, source_target_pairs={{0,4},{1,5},{2,6},{3,7},{4,8},{5,9},{6,10},{7,11},{8,12},{9,13},{1... | collective-permute-start | bytes 3145736 | tf_op jit(solution)/shard_map/ppermute | solution.py:29
  5.7 2.0 %copy-start.1 = (bf16[1,128,14336]{2,1,0:T(8,128)(2,1)S(1)}, bf16[1,128,14336]{2,1,0:T(8,128)(2,1)}, u32[]{:S(2)}) copy-start(bf16[1,128,14336]{2,1,0:T(8,128)(2,1)} %refs_3_) | copy-start | bytes 11010052
  12.4 109.9 %copy-start.2 = (bf16[4,896,128]{2,1,0:T(8,128)(2,1)}, bf16[4,896,128]{2,1,0:T(8,128)(2,1)S(1)}, u32[]{:S(2)}) copy-start(bf16[4,896,128]{2,1,0:T(8,128)(2,1)S(1)} %get-tuple-element.83.refs_0_) | copy-start | bytes 2752516
  25.9 27.3 %collective-permute-start.3 = (bf16[1,128,4096]{2,1,0:T(8,128)(2,1)}, bf16[1,128,4096]{2,1,0:T(8,128)(2,1)S(1)}, u32[]{:S(2)}, u32[]{:S(2)}) collective-permute-start(bf16[1,128,4096]{2,1,0:T(8,128)(2,1)} %collective-permute-done.refs_12_), channel_id=1, source_target_pairs={{0,1},{1,2},{2,3},{3,0},{4,5},{5,6},{6,7},{7,4},{8,9},{9,10},{10,1... | collective-permute-start | bytes 3145736 | tf_op jit(solution)/shard_map/ppermute | solution.py:29
  29.6 24.8 %collective-permute-start.4 = (bf16[4,896,128]{2,1,0:T(8,128)(2,1)}, bf16[4,896,128]{2,1,0:T(8,128)(2,1)}, u32[]{:S(2)}, u32[]{:S(2)}) collective-permute-start(bf16[4,896,128]{2,1,0:T(8,128)(2,1)} %get-tuple-element.97), channel_id=1, source_target_pairs={{0,4},{1,5},{2,6},{3,7},{4,8},{5,9},{6,10},{7,11},{8,12},{9,13},{1... | collective-permute-start | bytes 2752520 | tf_op jit(solution)/shard_map/ppermute | solution.py:29
  31.2 23.5 %collective-permute-start.5 = (bf16[4,896,128]{2,1,0:T(8,128)(2,1)}, bf16[4,896,128]{2,1,0:T(8,128)(2,1)S(1)}, u32[]{:S(2)}, u32[]{:S(2)}) collective-permute-start(bf16[4,896,128]{2,1,0:T(8,128)(2,1)} %get-tuple-element.99), channel_id=1, source_target_pairs={{0,12},{1,13},{2,14},{3,15},{4,0},{5,1},{6,2},{7,3},{8,4},{9,5},{1... | collective-permute-start | bytes 2752520 | tf_op jit(solution)/shard_map/ppermute | solution.py:29
  32.9 44.4 %collective-permute-start.7 = (bf16[1,128,4096]{2,1,0:T(8,128)(2,1)}, bf16[1,128,4096]{2,1,0:T(8,128)(2,1)}, u32[]{:S(2)}, u32[]{:S(2)}) collective-permute-start(bf16[1,128,4096]{2,1,0:T(8,128)(2,1)} %collective-permute-done.1.refs_11_), channel_id=1, source_target_pairs={{0,12},{1,13},{2,14},{3,15},{4,0},{5,1},{6,2},{7,3},{8,4},{9,5},{1... | collective-permute-start | bytes 3145736 | tf_op jit(solution)/shard_map/ppermute | solution.py:29
  34.7 39.4 %collective-permute-start.6 = (bf16[4,896,128]{2,1,0:T(8,128)(2,1)}, bf16[4,896,128]{2,1,0:T(8,128)(2,1)}, u32[]{:S(2)}, u32[]{:S(2)}) collective-permute-start(bf16[4,896,128]{2,1,0:T(8,128)(2,1)} %get-tuple-element.102), channel_id=1, source_target_pairs={{0,4},{1,5},{2,6},{3,7},{4,8},{5,9},{6,10},{7,11},{8,12},{9,13},{1... | collective-permute-start | bytes 2752520 | tf_op jit(solution)/shard_map/ppermute | solution.py:29
  34.9 27.2 %all-to-all-start = ((f32[16,32,128]{2,1,0:T(8,128)}), f32[16,32,128]{2,1,0:T(8,128)S(1)}, u32[]{:S(2)}, u32[]{:S(2)}) async-start(f32[16,32,128]{2,1,0:T(8,128)} %bitcast.20), calls=%async_computation | async-start | bytes 524288 | tf_op jit(solution)/shard_map/all_to_all | solution.py:120
  54.7 1.6 copy-start.4
  54.7 39.1 %collective-permute-start.8 = (bf16[4,896,128]{2,1,0:T(8,128)(2,1)}, bf16[4,896,128]{2,1,0:T(8,128)(2,1)}, u32[]{:S(2)}, u32[]{:S(2)}) collective-permute-start(bf16[4,896,128]{2,1,0:T(8,128)(2,1)} %collective-permute-done.4), channel_id=1, source_target_pairs={{0,4},{1,5},{2,6},{3,7},{4,8},{5,9},{6,10},{7,11},{8,12},{9,13},{1... | collective-permute-start | bytes 2752520 | tf_op jit(solution)/shard_map/ppermute | solution.py:29
  56.3 43.5 %collective-permute-start.9 = (bf16[1,128,4096]{2,1,0:T(8,128)(2,1)}, bf16[1,128,4096]{2,1,0:T(8,128)(2,1)}, u32[]{:S(2)}, u32[]{:S(2)}) collective-permute-start(bf16[1,128,4096]{2,1,0:T(8,128)(2,1)} %collective-permute-done.refs_12_), channel_id=1, source_target_pairs={{0,12},{1,13},{2,14},{3,15},{4,0},{5,1},{6,2},{7,3},{8,4},{9,5},{1... | collective-permute-start | bytes 3145736 | tf_op jit(solution)/shard_map/ppermute | solution.py:29
  58.5 42.8 %collective-permute-start.10 = (bf16[1,128,4096]{2,1,0:T(8,128)(2,1)S(1)}, bf16[1,128,4096]{2,1,0:T(8,128)(2,1)S(1)}, u32[]{:S(2)}, u32[]{:S(2)}) collective-permute-start(bf16[1,128,4096]{2,1,0:T(8,128)(2,1)S(1)} %collective-permute-done.3.refs_3_), channel_id=1, source_target_pairs={{0,1},{1,2},{2,3},{3,0},{4,5},{5,6},{6,7},{7,4},{8,9},{9,10},{10,1... | collective-permute-start | bytes 3145736 | tf_op jit(solution)/shard_map/ppermute | solution.py:29
  77.3 42.1 %collective-permute-start.11 = (bf16[1,128,4096]{2,1,0:T(8,128)(2,1)}, bf16[1,128,4096]{2,1,0:T(8,128)(2,1)}, u32[]{:S(2)}, u32[]{:S(2)}) collective-permute-start(bf16[1,128,4096]{2,1,0:T(8,128)(2,1)} %collective-permute-done.refs_12_), channel_id=1, source_target_pairs={{0,4},{1,5},{2,6},{3,7},{4,8},{5,9},{6,10},{7,11},{8,12},{9,13},{1... | collective-permute-start | bytes 3145736 | tf_op jit(solution)/shard_map/ppermute | solution.py:29
  79.0 43.3 %collective-permute-start.12 = (bf16[1,128,4096]{2,1,0:T(8,128)(2,1)S(1)}, bf16[1,128,4096]{2,1,0:T(8,128)(2,1)}, u32[]{:S(2)}, u32[]{:S(2)}) collective-permute-start(bf16[1,128,4096]{2,1,0:T(8,128)(2,1)S(1)} %collective-permute-done.3.refs_3_), channel_id=1, source_target_pairs={{0,12},{1,13},{2,14},{3,15},{4,0},{5,1},{6,2},{7,3},{8,4},{9,5},{1... | collective-permute-start | bytes 3145736 | tf_op jit(solution)/shard_map/ppermute | solution.py:29
  96.7 25.5 %collective-permute-start.13 = (bf16[4,896,128]{2,1,0:T(8,128)(2,1)}, bf16[4,896,128]{2,1,0:T(8,128)(2,1)}, u32[]{:S(2)}, u32[]{:S(2)}) collective-permute-start(bf16[4,896,128]{2,1,0:T(8,128)(2,1)} %pad_maximum_fusion), channel_id=1, source_target_pairs={{0,1},{1,2},{2,3},{3,0},{4,5},{5,6},{6,7},{7,4},{8,9},{9,10},{10,1... | collective-permute-start | bytes 2752520 | tf_op jit(solution)/shard_map/ppermute | solution.py:29
  99.8 39.0 %collective-permute-start.14 = (bf16[1,128,4096]{2,1,0:T(8,128)(2,1)S(1)}, bf16[1,128,4096]{2,1,0:T(8,128)(2,1)}, u32[]{:S(2)}, u32[]{:S(2)}) collective-permute-start(bf16[1,128,4096]{2,1,0:T(8,128)(2,1)S(1)} %collective-permute-done.3.refs_3_), channel_id=1, source_target_pairs={{0,4},{1,5},{2,6},{3,7},{4,8},{5,9},{6,10},{7,11},{8,12},{9,13},{1... | collective-permute-start | bytes 3145736 | tf_op jit(solution)/shard_map/ppermute | solution.py:29
  101.3 43.4 %collective-permute-start.15 = (bf16[1,128,4096]{2,1,0:T(8,128)(2,1)}, bf16[1,128,4096]{2,1,0:T(8,128)(2,1)}, u32[]{:S(2)}, u32[]{:S(2)}) collective-permute-start(bf16[1,128,4096]{2,1,0:T(8,128)(2,1)} %collective-permute-done.9.refs_15_), channel_id=1, source_target_pairs={{0,12},{1,13},{2,14},{3,15},{4,0},{5,1},{6,2},{7,3},{8,4},{9,5},{1... | collective-permute-start | bytes 3145736 | tf_op jit(solution)/shard_map/ppermute | solution.py:29
  105.8 19.4 %all-to-all-start.1 = ((f32[16,32,128]{2,1,0:T(8,128)}), f32[16,32,128]{2,1,0:T(8,128)S(1)}, u32[]{:S(2)}, u32[]{:S(2)}) async-start(f32[16,32,128]{2,1,0:T(8,128)} %broadcast_in_dim.13), calls=%async_computation.1 | async-start | bytes 524288 | tf_op jit(solution)/shard_map/all_to_all | solution.py:134
  122.2 42.3 %collective-permute-start.16 = (bf16[1,128,4096]{2,1,0:T(8,128)(2,1)S(1)}, bf16[1,128,4096]{2,1,0:T(8,128)(2,1)}, u32[]{:S(2)}, u32[]{:S(2)}) collective-permute-start(bf16[1,128,4096]{2,1,0:T(8,128)(2,1)S(1)} %collective-permute-done.10.refs_4_), channel_id=1, source_target_pairs={{0,12},{1,13},{2,14},{3,15},{4,0},{5,1},{6,2},{7,3},{8,4},{9,5},{1... | collective-permute-start | bytes 3145736 | tf_op jit(solution)/shard_map/ppermute | solution.py:29
  125.1 42.5 %collective-permute-start.17 = (bf16[4,896,128]{2,1,0:T(8,128)(2,1)}, bf16[4,896,128]{2,1,0:T(8,128)(2,1)S(1)}, u32[]{:S(2)}, u32[]{:S(2)}) collective-permute-start(bf16[4,896,128]{2,1,0:T(8,128)(2,1)} %pad_maximum_fusion.1), channel_id=1, source_target_pairs={{0,2},{1,3},{2,0},{3,1},{4,6},{5,7},{6,4},{7,5},{8,10},{9,11},{10,... | collective-permute-start | bytes 2752520 | tf_op jit(solution)/shard_map/ppermute | solution.py:29
  125.1 50.8 %collective-permute-start.19 = (bf16[1,128,4096]{2,1,0:T(8,128)(2,1)S(1)}, bf16[1,128,4096]{2,1,0:T(8,128)(2,1)}, u32[]{:S(2)}, u32[]{:S(2)}) collective-permute-start(bf16[1,128,4096]{2,1,0:T(8,128)(2,1)S(1)} %collective-permute-done.10.refs_4_), channel_id=1, source_target_pairs={{0,4},{1,5},{2,6},{3,7},{4,8},{5,9},{6,10},{7,11},{8,12},{9,13},{1... | collective-permute-start | bytes 3145736 | tf_op jit(solution)/shard_map/ppermute | solution.py:29
  144.7 36.6 %collective-permute-start.18 = (bf16[1,128,4096]{2,1,0:T(8,128)(2,1)}, bf16[1,128,4096]{2,1,0:T(8,128)(2,1)S(1)}, u32[]{:S(2)}, u32[]{:S(2)}) collective-permute-start(bf16[1,128,4096]{2,1,0:T(8,128)(2,1)} %collective-permute-done.14.refs_4_), channel_id=1, source_target_pairs={{0,4},{1,5},{2,6},{3,7},{4,8},{5,9},{6,10},{7,11},{8,12},{9,13},{1... | collective-permute-start | bytes 3145736 | tf_op jit(solution)/shard_map/ppermute | solution.py:29
  146.3 1.2 copy-start.3
  147.5 1.2 copy-start.5
  148.6 1.2 copy-start.6
  149.9 17.6 %copy-start.7 = (bf16[1,896,128]{2,1,0:T(8,128)(2,1)S(1)}, bf16[1,896,128]{2,1,0:T(8,128)(2,1)}, u32[]{:S(2)}) copy-start(bf16[1,896,128]{2,1,0:T(8,128)(2,1)} %get-tuple-element.165) | copy-start | bytes 688132
  149.9 17.6 %copy-start.8 = (bf16[1,896,128]{2,1,0:T(8,128)(2,1)S(1)}, bf16[1,896,128]{2,1,0:T(8,128)(2,1)}, u32[]{:S(2)}) copy-start(bf16[1,896,128]{2,1,0:T(8,128)(2,1)} %get-tuple-element.159) | copy-start | bytes 688132
  149.9 17.6 %copy-start.9 = (bf16[1,896,128]{2,1,0:T(8,128)(2,1)S(1)}, bf16[1,896,128]{2,1,0:T(8,128)(2,1)}, u32[]{:S(2)}) copy-start(bf16[1,896,128]{2,1,0:T(8,128)(2,1)} %get-tuple-element.162) | copy-start | bytes 688132
  149.9 17.6 %copy-start.10 = (bf16[1,896,128]{2,1,0:T(8,128)(2,1)S(1)}, bf16[1,896,128]{2,1,0:T(8,128)(2,1)}, u32[]{:S(2)}) copy-start(bf16[1,896,128]{2,1,0:T(8,128)(2,1)} %get-tuple-element.167) | copy-start | bytes 688132
  164.5 24.5 %collective-permute-start.21 = (bf16[1,128,4096]{2,1,0:T(8,128)(2,1)}, bf16[1,128,4096]{2,1,0:T(8,128)(2,1)S(1)}, u32[]{:S(2)}, u32[]{:S(2)}) collective-permute-start(bf16[1,128,4096]{2,1,0:T(8,128)(2,1)} %collective-permute-done.16.refs_7_), channel_id=1, source_target_pairs={{0,12},{1,13},{2,14},{3,15},{4,0},{5,1},{6,2},{7,3},{8,4},{9,5},{1... | collective-permute-start | bytes 3145736 | tf_op jit(solution)/shard_map/ppermute | solution.py:29
  167.6 21.4 %collective-permute-start.20 = (bf16[4,896,128]{2,1,0:T(8,128)(2,1)S(1)}, bf16[4,896,128]{2,1,0:T(8,128)(2,1)S(1)}, u32[]{:S(2)}, u32[]{:S(2)}) collective-permute-start(bf16[4,896,128]{2,1,0:T(8,128)(2,1)S(1)} %pad_maximum_fusion.2), channel_id=1, source_target_pairs={{0,3},{1,0},{2,1},{3,2},{4,7},{5,4},{6,5},{7,6},{8,11},{9,8},{10,9... | collective-permute-start | bytes 2752520 | tf_op jit(solution)/shard_map/ppermute | solution.py:29

commit v3 on v2

--- a/solution.py
+++ b/solution.py
@@ -83,13 +83,16 @@
     alias = {}
     if total is not None:
         operands.append(total)
-        in_specs.append(tile)
+        in_specs.append(pl.BlockSpec(memory_space=pltpu.VMEM) if final else tile)
         if not final:
             alias = {n + m + 1: 0}
 
     def kernel(*refs):
         out_ref, token_ref, packed = refs[-3:]
         extra = refs[n + m + 1] if total is not None else None
+        if final:
+            first = pl.multiple_of(pl.program_id(0) * width, width)
+            extra = extra.at[:, :, pl.ds(first, width)]
         matmul_kernel(refs[:n], refs[n : n + m], extra, out_ref, packed)
         token_ref[...] = jnp.zeros_like(token_ref)
 
@@ -179,7 +182,7 @@
             part = ("b", "p", "f", "m")[d] + str(k)
             right = [env[part]] if part in env else [env[part + "y"], env[part + "z"]]
             blocks.append((env[array], row, right))
-        env[name], env["token"] = matmul(blocks, env["token"], total, final)
+        env[name], env["token"] = matmul(blocks, env["token"], total, final, 1024 if final else 512)
 
     every = range(NY)
     event([], [along(1), down(0), up(0)])

time: 200 us -> 198 us (0.990)
  Pallas kernels: 40 us -> 37.9 us
    pallas_call x4, Pallas kernels: 35.4 us -> 33.3 us  [matmul(): pl.pallas_call(kernel, grid=(COLUMNS // width,), in_specs=in_specs, out_s...]
where the time goes in v3:
time: 198 us; the launch traced here: 197 us
  waiting for transfers between devices  82.9 us (42%)
  starting transfers between devices  53.8 us (27%)
  Pallas kernels  37.9 us (19%)
  local copies, waits for them, and re-layouts  15.2 us (8%)
  other arithmetic  6.49 us (3%)
    ppermute x22, waiting for transfers between devices, fsdp_send(): return lax.ppermute(array, 'fsdp', shift(dy, dz))  82.9 us
    ppermute x22, starting transfers between devices, fsdp_send(): return lax.ppermute(array, 'fsdp', shift(dy, dz))  34.5 us
    pallas_call x4, Pallas kernels, matmul(): pl.pallas_call(kernel, grid=(COLUMNS // width,), in_specs=in_specs, out_s...  33.3 us
    all_to_all x1, starting transfers between devices, reduce_shares(): return lax.all_to_all(pieces, 'replica', 0, 0, tiled=True)  9.68 us
    all_to_all x1, starting transfers between devices, hand_out(): return lax.all_to_all(copies, 'replica', 0, 0, tiled=True)  9.68 us
    slice x5, local copies, waits for them, and re-layouts, packed(): return jnp.stack([env[f'R{d}'][s] for d in near])  7.52 us
    unnamed x23, local copies, waits for them, and re-layouts  6.35 us
    pallas_call x1, Pallas kernels, activate(): pl.pallas_call(activate_kernel, grid_spec=pltpu.PrefetchScalarGridSpec(nu...  4.62 us
  transfers between devices with their start and end apart: 24, of which 15 were waited for; matrix products, arithmetic and copies ran while one was open for 8% of the time, Pallas kernels for 15%

profile of v3, /device:TPU:224, one launch (start us, length us, event | category | flops | bytes accessed | tf_op | source)
XLA Modules:
  0.0 197.1 jit_solution(9788133253987824186)
XLA Ops:
  0.6 0.0 copy-start
  0.6 2.0 %collective-permute-start = (bf16[1,128,4096]{2,1,0:T(8,128)(2,1)}, bf16[1,128,4096]{2,1,0:T(8,128)(2,1)}, u32[]{:S(2)}, u32[]{:S(2)}) collective-permute-start(bf16[1,128,4096]{2,1,0:T(8,128)(2,1)} %refs_8_.1), channel_id=1, source_target_pairs={{0,1},{1,2},{2,3},{3,0},{4,5},{5,6},{6,7},{7,4},{8,9},{9,10},{10,1... | collective-permute-start | bytes 3145736 | tf_op jit(solution)/shard_map/ppermute | solution.py:29
  2.6 3.0 %collective-permute-start.1 = (bf16[1,128,4096]{2,1,0:T(8,128)(2,1)}, bf16[1,128,4096]{2,1,0:T(8,128)(2,1)}, u32[]{:S(2)}, u32[]{:S(2)}) collective-permute-start(bf16[1,128,4096]{2,1,0:T(8,128)(2,1)} %refs_8_.1), channel_id=1, source_target_pairs={{0,12},{1,13},{2,14},{3,15},{4,0},{5,1},{6,2},{7,3},{8,4},{9,5},{1... | collective-permute-start | bytes 3145736 | tf_op jit(solution)/shard_map/ppermute | solution.py:29
  5.6 0.1 pad_add_fusion.place_ref
  5.7 2.0 %copy-done.1 = bf16[1,128,14336]{2,1,0:T(8,128)(2,1)S(1)} copy-done((bf16[1,128,14336]{2,1,0:T(8,128)(2,1)S(1)}, bf16[1,128,14336]{2,1,0:T(8,128)(2,1)}, u32[]{:S(2)}) %copy-start.1) | copy-done | bytes 3670040
  7.8 4.6 %shard_map.76 = (bf16[4,896,128]{2,1,0:T(8,128)(2,1)S(1)}, bf16[4,896,128]{2,1,0:T(8,128)(2,1)}, bf16[4,896,128]{2,1,0:T(8,128)(2,1)}, bf16[4,896,128]{2,1,0:T(8,128)(2,1)}) custom-call(s32[2]{0:T(128)S(1)} %pad_add_fusion.place_ref, bf16[1,128,14336]{2,1,0:T(8,128)(2,1)S(1)} %copy-done.1, bf16[1,128,14336]{2,1,0:T(8,128)(2,1)S(1)} %copy-done.1, ...), custom_call_target="tpu_custom_call" | custom-call | tf_op jit(solution)/shard_map/pallas_call | solution.py:43
  12.4 13.6 %collective-permute-done.refs_12_ = bf16[1,128,4096]{2,1,0:T(8,128)(2,1)} collective-permute-done((bf16[1,128,4096]{2,1,0:T(8,128)(2,1)}, bf16[1,128,4096]{2,1,0:T(8,128)(2,1)}, u32[]{:S(2)}, u32[]{:S(2)}) %collective-permute-start) | collective-permute-done | bytes 1048608 | tf_op jit(solution)/shard_map/ppermute | solution.py:29
  25.9 3.7 %collective-permute-start.3 = (bf16[1,128,4096]{2,1,0:T(8,128)(2,1)}, bf16[1,128,4096]{2,1,0:T(8,128)(2,1)S(1)}, u32[]{:S(2)}, u32[]{:S(2)}) collective-permute-start(bf16[1,128,4096]{2,1,0:T(8,128)(2,1)} %collective-permute-done.refs_12_), channel_id=1, source_target_pairs={{0,1},{1,2},{2,3},{3,0},{4,5},{5,6},{6,7},{7,4},{8,9},{9,10},{10,1... | collective-permute-start | bytes 3145736 | tf_op jit(solution)/shard_map/ppermute | solution.py:29
  29.6 1.6 collective-permute-start.4
  31.2 1.7 collective-permute-start.5
  32.9 0.0 collective-permute-done.2.refs_9_
  32.9 1.8 collective-permute-start.7
  34.7 0.2 collective-permute-start.6
  34.9 9.7 %all-to-all-start = ((f32[16,32,128]{2,1,0:T(8,128)}), f32[16,32,128]{2,1,0:T(8,128)S(1)}, u32[]{:S(2)}, u32[]{:S(2)}) async-start(f32[16,32,128]{2,1,0:T(8,128)} %bitcast.20), calls=%async_computation | async-start | bytes 524288 | tf_op jit(solution)/shard_map/all_to_all | solution.py:123
  44.6 0.6 constant_dynamic-slice_fusion
  45.2 8.0 %collective-permute-done.3.refs_3_ = bf16[1,128,4096]{2,1,0:T(8,128)(2,1)S(1)} collective-permute-done((bf16[1,128,4096]{2,1,0:T(8,128)(2,1)}, bf16[1,128,4096]{2,1,0:T(8,128)(2,1)S(1)}, u32[]{:S(2)}, u32[]{:S(2)}) %collective-permute-start.3) | collective-permute-done | bytes 1048608 | tf_op jit(solution)/shard_map/ppermute | solution.py:29
  53.2 1.2 collective-permute-done.4
  54.4 0.3 collective-permute-done.5.refs_3_
  54.7 1.6 collective-permute-start.8
  56.3 2.2 %collective-permute-start.9 = (bf16[1,128,4096]{2,1,0:T(8,128)(2,1)}, bf16[1,128,4096]{2,1,0:T(8,128)(2,1)}, u32[]{:S(2)}, u32[]{:S(2)}) collective-permute-start(bf16[1,128,4096]{2,1,0:T(8,128)(2,1)} %collective-permute-done.refs_12_), channel_id=1, source_target_pairs={{0,12},{1,13},{2,14},{3,15},{4,0},{5,1},{6,2},{7,3},{8,4},{9,5},{1... | collective-permute-start | bytes 3145736 | tf_op jit(solution)/shard_map/ppermute | solution.py:29
  58.5 2.7 %collective-permute-start.10 = (bf16[1,128,4096]{2,1,0:T(8,128)(2,1)S(1)}, bf16[1,128,4096]{2,1,0:T(8,128)(2,1)S(1)}, u32[]{:S(2)}, u32[]{:S(2)}) collective-permute-start(bf16[1,128,4096]{2,1,0:T(8,128)(2,1)S(1)} %collective-permute-done.3.refs_3_), channel_id=1, source_target_pairs={{0,1},{1,2},{2,3},{3,0},{4,5},{5,6},{6,7},{7,4},{8,9},{9,10},{10,1... | collective-permute-start | bytes 3145736 | tf_op jit(solution)/shard_map/ppermute | solution.py:29
  61.2 0.9 fusion.4
  62.1 0.0 all-to-all-done
  62.1 12.0 %collective-permute-done.6.refs_1_ = bf16[4,896,128]{2,1,0:T(8,128)(2,1)} collective-permute-done((bf16[4,896,128]{2,1,0:T(8,128)(2,1)}, bf16[4,896,128]{2,1,0:T(8,128)(2,1)}, u32[]{:S(2)}, u32[]{:S(2)}) %collective-permute-start.6) | collective-permute-done | bytes 917536 | tf_op jit(solution)/shard_map/ppermute | solution.py:29
  74.1 3.2 %collective-permute-done.7.refs_10_ = bf16[1,128,4096]{2,1,0:T(8,128)(2,1)} collective-permute-done((bf16[1,128,4096]{2,1,0:T(8,128)(2,1)}, bf16[1,128,4096]{2,1,0:T(8,128)(2,1)}, u32[]{:S(2)}, u32[]{:S(2)}) %collective-permute-start.7) | collective-permute-done | bytes 1048608 | tf_op jit(solution)/shard_map/ppermute | solution.py:29
  77.3 1.7 collective-permute-start.11
  79.0 1.7 collective-permute-start.12
  80.6 2.0 fusion.5
  82.6 2.0 %fusion.7 = (bf16[1,896,128]{2,1,0:T(8,128)(2,1)}, bf16[1,896,128]{2,1,0:T(8,128)(2,1)}, bf16[1,896,128]{2,1,0:T(8,128)(2,1)S(1)}) fusion(bf16[4,896,128]{2,1,0:T(8,128)(2,1)} %copy-done.4), kind=kLoop, calls=%fused_computation.16 | loop fusion | bytes 1376256 | tf_op jit(solution)/shard_map/slice | solution.py:170
  84.6 9.2 %collective-permute-done.8.refs_2_ = bf16[4,896,128]{2,1,0:T(8,128)(2,1)} collective-permute-done((bf16[4,896,128]{2,1,0:T(8,128)(2,1)}, bf16[4,896,128]{2,1,0:T(8,128)(2,1)}, u32[]{:S(2)}, u32[]{:S(2)}) %collective-permute-start.8) | collective-permute-done | bytes 917536 | tf_op jit(solution)/shard_map/ppermute | solution.py:29
  93.8 1.0 slice.48
  94.7 2.0 %pad_maximum_fusion = bf16[4,896,128]{2,1,0:T(8,128)(2,1)} fusion(bf16[1,896,128]{2,1,0:T(8,128)(2,1)S(1)} %get-tuple-element.169, bf16[1,896,128]{2,1,0:T(8,128)(2,1)S(1)} %slice.48, bf16[1,896,128]{2,1,0:T(8,128)(2,1)S(1)} %get-tuple-element.164, bf16[1,896,128]{2,1,0:T(8,128)(2,1)} %get-tuple-element.161), kind=kLoop, calls=%fused_computation | loop fusion | flops 1376256 | bytes 1835008 | tf_op jit(solution)/shard_map/stack | solution.py:170
  96.7 0.0 collective-permute-start.13
  96.7 3.0 %collective-permute-done.9.refs_15_ = bf16[1,128,4096]{2,1,0:T(8,128)(2,1)} collective-permute-done((bf16[1,128,4096]{2,1,0:T(8,128)(2,1)}, bf16[1,128,4096]{2,1,0:T(8,128)(2,1)}, u32[]{:S(2)}, u32[]{:S(2)}) %collective-permute-start.9) | collective-permute-done | bytes 1048608 | tf_op jit(solution)/shard_map/ppermute | solution.py:29
  99.8 1.6 collective-permute-start.14
  101.3 1.7 collective-permute-start.15
  103.0 1.4 fusion.3
  104.3 0.7 fusion.2
  105.1 0.7 broadcast_in_dim.13
  105.8 9.7 %all-to-all-start.1 = ((f32[16,32,128]{2,1,0:T(8,128)}), f32[16,32,128]{2,1,0:T(8,128)S(1)}, u32[]{:S(2)}, u32[]{:S(2)}) async-start(f32[16,32,128]{2,1,0:T(8,128)} %broadcast_in_dim.13), calls=%async_computation.1 | async-start | bytes 524288 | tf_op jit(solution)/shard_map/all_to_all | solution.py:137
  115.5 1.8 fusion.6
  117.3 2.2 %pad_maximum_fusion.1 = bf16[4,896,128]{2,1,0:T(8,128)(2,1)} fusion(bf16[1,896,128]{2,1,0:T(8,128)(2,1)} %get-tuple-element.168, bf16[1,896,128]{2,1,0:T(8,128)(2,1)S(1)} %get-tuple-element.166, bf16[1,896,128]{2,1,0:T(8,128)(2,1)} %get-tuple-element.163, bf16[1,896,128]{2,1,0:T(8,128)(2,1)} %get-tuple-element.160), kind=kLoop, calls=%fused_computation.1 | loop fusion | flops 1376256 | bytes 1835008 | tf_op jit(solution)/shard_map/stack | solution.py:170
  119.5 0.0 collective-permute-done.11.refs_13_
  119.5 2.8 %collective-permute-done.12.refs_5_ = bf16[1,128,4096]{2,1,0:T(8,128)(2,1)} collective-permute-done((bf16[1,128,4096]{2,1,0:T(8,128)(2,1)S(1)}, bf16[1,128,4096]{2,1,0:T(8,128)(2,1)}, u32[]{:S(2)}, u32[]{:S(2)}) %collective-permute-start.12) | collective-permute-done | bytes 1048608 | tf_op jit(solution)/shard_map/ppermute | solution.py:29
  122.2 0.0 collective-permute-done.13.refs_4_.refs_5_.refs_6_.refs_7_
  122.2 2.9 %collective-permute-start.16 = (bf16[1,128,4096]{2,1,0:T(8,128)(2,1)S(1)}, bf16[1,128,4096]{2,1,0:T(8,128)(2,1)}, u32[]{:S(2)}, u32[]{:S(2)}) collective-permute-start(bf16[1,128,4096]{2,1,0:T(8,128)(2,1)S(1)} %collective-permute-done.10.refs_4_), channel_id=1, source_target_pairs={{0,12},{1,13},{2,14},{3,15},{4,0},{5,1},{6,2},{7,3},{8,4},{9,5},{1... | collective-permute-start | bytes 3145736 | tf_op jit(solution)/shard_map/ppermute | solution.py:29
  125.1 0.1 all-to-all-done.1
  125.2 13.5 %collective-permute-done.14.refs_4_ = bf16[1,128,4096]{2,1,0:T(8,128)(2,1)} collective-permute-done((bf16[1,128,4096]{2,1,0:T(8,128)(2,1)S(1)}, bf16[1,128,4096]{2,1,0:T(8,128)(2,1)}, u32[]{:S(2)}, u32[]{:S(2)}) %collective-permute-start.14) | collective-permute-done | bytes 1048608 | tf_op jit(solution)/shard_map/ppermute | solution.py:29
  138.7 6.0 %collective-permute-done.15.refs_14_ = bf16[1,128,4096]{2,1,0:T(8,128)(2,1)} collective-permute-done((bf16[1,128,4096]{2,1,0:T(8,128)(2,1)}, bf16[1,128,4096]{2,1,0:T(8,128)(2,1)}, u32[]{:S(2)}, u32[]{:S(2)}) %collective-permute-start.15) | collective-permute-done | bytes 1048608 | tf_op jit(solution)/shard_map/ppermute | solution.py:29
  144.7 1.6 collective-permute-start.18
  146.3 1.2 copy-done.3
  147.5 1.2 copy-done.5
  148.6 1.2 copy-done.6
  149.9 12.5 %shard_map.77 = (f32[1,896,4096]{2,1,0:T(8,128)S(1)}, f32[8,128]{1,0:T(8,128)S(1)}) custom-call(bf16[4,896,128]{2,1,0:T(8,128)(2,1)S(1)} %copy-done.3, bf16[4,896,128]{2,1,0:T(8,128)(2,1)} %collective-permute-done.6.refs_1_, bf16[4,896,128]{2,1,0:T(8,128)(2,1)} %collective-permute-done.8.refs_2_, bf16[4,896,128]{2,1,0:T(8,128)(2,1)S(1)} %copy-done.5, ...), custom_call_target="tpu_custom_call" | custom-call | flops 7516192768 | bytes 24903680 | tf_op jit(solution)/shard_map/pallas_call | solution.py:99
  162.4 2.2 %collective-permute-done.16.refs_7_ = bf16[1,128,4096]{2,1,0:T(8,128)(2,1)} collective-permute-done((bf16[1,128,4096]{2,1,0:T(8,128)(2,1)S(1)}, bf16[1,128,4096]{2,1,0:T(8,128)(2,1)}, u32[]{:S(2)}, u32[]{:S(2)}) %collective-permute-start.16) | collective-permute-done | bytes 1048608 | tf_op jit(solution)/shard_map/ppermute | solution.py:29
  164.5 2.9 %collective-permute-start.21 = (bf16[1,128,4096]{2,1,0:T(8,128)(2,1)}, bf16[1,128,4096]{2,1,0:T(8,128)(2,1)S(1)}, u32[]{:S(2)}, u32[]{:S(2)}) collective-permute-start(bf16[1,128,4096]{2,1,0:T(8,128)(2,1)} %collective-permute-done.16.refs_7_), channel_id=1, source_target_pairs={{0,12},{1,13},{2,14},{3,15},{4,0},{5,1},{6,2},{7,3},{8,4},{9,5},{1... | collective-permute-start | bytes 3145736 | tf_op jit(solution)/shard_map/ppermute | solution.py:29
  167.5 0.1 pad_maximum_fusion.2
  167.6 0.1 collective-permute-start.20
  167.7 8.2 %shard_map.78 = (f32[1,896,4096]{2,1,0:T(8,128)S(1)}, f32[8,128]{1,0:T(8,128)S(1)}) custom-call(bf16[4,896,128]{2,1,0:T(8,128)(2,1)S(1)} %collective-permute-done.17.refs_0_.refs_1_.refs_2_, bf16[4,896,128]{2,1,0:T(8,128)(2,1)S(1)} %collective-permute-done.17.refs_0_.refs_1_.refs_2_, ...), custom_call_target="tpu_custom_call", output_to_operand_aliasing={{0}: (7, {})} | custom-call | flops 2818572288 | bytes 18513920 | tf_op jit(solution)/shard_map/pallas_call | solution.py:99
  175.9 5.3 %collective-permute-done.18.refs_1_ = bf16[1,128,4096]{2,1,0:T(8,128)(2,1)S(1)} collective-permute-done((bf16[1,128,4096]{2,1,0:T(8,128)(2,1)}, bf16[1,128,4096]{2,1,0:T(8,128)(2,1)S(1)}, u32[]{:S(2)}, u32[]{:S(2)}) %collective-permute-start.18) | collective-permute-done | bytes 1048608 | tf_op jit(solution)/shard_map/ppermute | solution.py:29
  181.3 5.2 %shard_map.79 = (f32[1,896,4096]{2,1,0:T(8,128)S(1)}, f32[8,128]{1,0:T(8,128)S(1)}) custom-call(bf16[4,896,128]{2,1,0:T(8,128)(2,1)S(1)} %collective-permute-done.17.refs_0_.refs_1_.refs_2_, bf16[1,128,4096]{2,1,0:T(8,128)(2,1)S(1)} %collective-permute-done.18.refs_1_, f32[8,128]{1,0:T(8,128)S(1)} %get-tuple-element.145.refs_2_, ...), custom_call_target="tpu_custom_call", output_to_operand_aliasing={{0}: (3, {})} | custom-call | flops 939524096 | bytes 15958016 | tf_op jit(solution)/shard_map/pallas_call | solution.py:99
  186.4 2.6 %collective-permute-done.20.refs_0_.refs_1_.refs_2_.refs_3_ = bf16[4,896,128]{2,1,0:T(8,128)(2,1)S(1)} collective-permute-done((bf16[4,896,128]{2,1,0:T(8,128)(2,1)S(1)}, bf16[4,896,128]{2,1,0:T(8,128)(2,1)S(1)}, u32[]{:S(2)}, u32[]{:S(2)}) %collective-permute-start.20) | collective-permute-done | bytes 917536 | tf_op jit(solution)/shard_map/ppermute | solution.py:29
  189.0 7.4 %shard_map.80 = (bf16[1,896,4096]{2,1,0:T(8,128)(2,1)}, f32[8,128]{1,0:T(8,128)}) custom-call(bf16[4,896,128]{2,1,0:T(8,128)(2,1)S(1)} %collective-permute-done.20.refs_0_.refs_1_.refs_2_.refs_3_, bf16[4,896,128]{2,1,0:T(8,128)(2,1)S(1)} %collective-permute-done.20.refs_0_.refs_1_.refs_2_.refs_3_, ...), custom_call_target="tpu_custom_call" | custom-call | flops 3758096384 | bytes 19791872 | tf_op jit(solution)/shard_map/pallas_call | solution.py:99
  196.4 0.7 copy.13
  (28 shorter events, 0.1 us)
Async XLA Ops:
  0.6 44.0 %copy-start = (f32[1,65536]{1,0:T(1,128)S(1)}, f32[1,65536]{1,0:T(1,128)}, u32[]{:S(2)}) copy-start(f32[1,65536]{1,0:T(1,128)} %param.8) | copy-start | bytes 786436
  0.6 25.3 %collective-permute-start = (bf16[1,128,4096]{2,1,0:T(8,128)(2,1)}, bf16[1,128,4096]{2,1,0:T(8,128)(2,1)}, u32[]{:S(2)}, u32[]{:S(2)}) collective-permute-start(bf16[1,128,4096]{2,1,0:T(8,128)(2,1)} %refs_8_.1), channel_id=1, source_target_pairs={{0,1},{1,2},{2,3},{3,0},{4,5},{5,6},{6,7},{7,4},{8,9},{9,10},{10,1... | collective-permute-start | bytes 3145736 | tf_op jit(solution)/shard_map/ppermute | solution.py:29
  2.6 30.3 %collective-permute-start.1 = (bf16[1,128,4096]{2,1,0:T(8,128)(2,1)}, bf16[1,128,4096]{2,1,0:T(8,128)(2,1)}, u32[]{:S(2)}, u32[]{:S(2)}) collective-permute-start(bf16[1,128,4096]{2,1,0:T(8,128)(2,1)} %refs_8_.1), channel_id=1, source_target_pairs={{0,12},{1,13},{2,14},{3,15},{4,0},{5,1},{6,2},{7,3},{8,4},{9,5},{1... | collective-permute-start | bytes 3145736 | tf_op jit(solution)/shard_map/ppermute | solution.py:29
  5.6 27.2 %collective-permute-start.2 = (bf16[1,128,4096]{2,1,0:T(8,128)(2,1)}, bf16[1,128,4096]{2,1,0:T(8,128)(2,1)}, u32[]{:S(2)}, u32[]{:S(2)}) collective-permute-start(bf16[1,128,4096]{2,1,0:T(8,128)(2,1)} %refs_8_.1), channel_id=1, source_target_pairs={{0,4},{1,5},{2,6},{3,7},{4,8},{5,9},{6,10},{7,11},{8,12},{9,13},{1... | collective-permute-start | bytes 3145736 | tf_op jit(solution)/shard_map/ppermute | solution.py:29
  5.7 2.0 %copy-start.1 = (bf16[1,128,14336]{2,1,0:T(8,128)(2,1)S(1)}, bf16[1,128,14336]{2,1,0:T(8,128)(2,1)}, u32[]{:S(2)}) copy-start(bf16[1,128,14336]{2,1,0:T(8,128)(2,1)} %refs_3_) | copy-start | bytes 11010052
  12.4 109.9 %copy-start.2 = (bf16[4,896,128]{2,1,0:T(8,128)(2,1)}, bf16[4,896,128]{2,1,0:T(8,128)(2,1)S(1)}, u32[]{:S(2)}) copy-start(bf16[4,896,128]{2,1,0:T(8,128)(2,1)S(1)} %get-tuple-element.83.refs_0_) | copy-start | bytes 2752516
  25.9 27.3 %collective-permute-start.3 = (bf16[1,128,4096]{2,1,0:T(8,128)(2,1)}, bf16[1,128,4096]{2,1,0:T(8,128)(2,1)S(1)}, u32[]{:S(2)}, u32[]{:S(2)}) collective-permute-start(bf16[1,128,4096]{2,1,0:T(8,128)(2,1)} %collective-permute-done.refs_12_), channel_id=1, source_target_pairs={{0,1},{1,2},{2,3},{3,0},{4,5},{5,6},{6,7},{7,4},{8,9},{9,10},{10,1... | collective-permute-start | bytes 3145736 | tf_op jit(solution)/shard_map/ppermute | solution.py:29
  29.6 24.8 %collective-permute-start.4 = (bf16[4,896,128]{2,1,0:T(8,128)(2,1)}, bf16[4,896,128]{2,1,0:T(8,128)(2,1)}, u32[]{:S(2)}, u32[]{:S(2)}) collective-permute-start(bf16[4,896,128]{2,1,0:T(8,128)(2,1)} %get-tuple-element.97), channel_id=1, source_target_pairs={{0,4},{1,5},{2,6},{3,7},{4,8},{5,9},{6,10},{7,11},{8,12},{9,13},{1... | collective-permute-start | bytes 2752520 | tf_op jit(solution)/shard_map/ppermute | solution.py:29
  31.2 23.5 %collective-permute-start.5 = (bf16[4,896,128]{2,1,0:T(8,128)(2,1)}, bf16[4,896,128]{2,1,0:T(8,128)(2,1)S(1)}, u32[]{:S(2)}, u32[]{:S(2)}) collective-permute-start(bf16[4,896,128]{2,1,0:T(8,128)(2,1)} %get-tuple-element.99), channel_id=1, source_target_pairs={{0,12},{1,13},{2,14},{3,15},{4,0},{5,1},{6,2},{7,3},{8,4},{9,5},{1... | collective-permute-start | bytes 2752520 | tf_op jit(solution)/shard_map/ppermute | solution.py:29
  32.9 44.4 %collective-permute-start.7 = (bf16[1,128,4096]{2,1,0:T(8,128)(2,1)}, bf16[1,128,4096]{2,1,0:T(8,128)(2,1)}, u32[]{:S(2)}, u32[]{:S(2)}) collective-permute-start(bf16[1,128,4096]{2,1,0:T(8,128)(2,1)} %collective-permute-done.1.refs_11_), channel_id=1, source_target_pairs={{0,12},{1,13},{2,14},{3,15},{4,0},{5,1},{6,2},{7,3},{8,4},{9,5},{1... | collective-permute-start | bytes 3145736 | tf_op jit(solution)/shard_map/ppermute | solution.py:29
  34.7 39.4 %collective-permute-start.6 = (bf16[4,896,128]{2,1,0:T(8,128)(2,1)}, bf16[4,896,128]{2,1,0:T(8,128)(2,1)}, u32[]{:S(2)}, u32[]{:S(2)}) collective-permute-start(bf16[4,896,128]{2,1,0:T(8,128)(2,1)} %get-tuple-element.102), channel_id=1, source_target_pairs={{0,4},{1,5},{2,6},{3,7},{4,8},{5,9},{6,10},{7,11},{8,12},{9,13},{1... | collective-permute-start | bytes 2752520 | tf_op jit(solution)/shard_map/ppermute | solution.py:29
  34.9 27.2 %all-to-all-start = ((f32[16,32,128]{2,1,0:T(8,128)}), f32[16,32,128]{2,1,0:T(8,128)S(1)}, u32[]{:S(2)}, u32[]{:S(2)}) async-start(f32[16,32,128]{2,1,0:T(8,128)} %bitcast.20), calls=%async_computation | async-start | bytes 524288 | tf_op jit(solution)/shard_map/all_to_all | solution.py:123
  54.7 1.6 copy-start.4
  54.7 39.1 %collective-permute-start.8 = (bf16[4,896,128]{2,1,0:T(8,128)(2,1)}, bf16[4,896,128]{2,1,0:T(8,128)(2,1)}, u32[]{:S(2)}, u32[]{:S(2)}) collective-permute-start(bf16[4,896,128]{2,1,0:T(8,128)(2,1)} %collective-permute-done.4), channel_id=1, source_target_pairs={{0,4},{1,5},{2,6},{3,7},{4,8},{5,9},{6,10},{7,11},{8,12},{9,13},{1... | collective-permute-start | bytes 2752520 | tf_op jit(solution)/shard_map/ppermute | solution.py:29
  56.3 43.5 %collective-permute-start.9 = (bf16[1,128,4096]{2,1,0:T(8,128)(2,1)}, bf16[1,128,4096]{2,1,0:T(8,128)(2,1)}, u32[]{:S(2)}, u32[]{:S(2)}) collective-permute-start(bf16[1,128,4096]{2,1,0:T(8,128)(2,1)} %collective-permute-done.refs_12_), channel_id=1, source_target_pairs={{0,12},{1,13},{2,14},{3,15},{4,0},{5,1},{6,2},{7,3},{8,4},{9,5},{1... | collective-permute-start | bytes 3145736 | tf_op jit(solution)/shard_map/ppermute | solution.py:29
  58.5 42.8 %collective-permute-start.10 = (bf16[1,128,4096]{2,1,0:T(8,128)(2,1)S(1)}, bf16[1,128,4096]{2,1,0:T(8,128)(2,1)S(1)}, u32[]{:S(2)}, u32[]{:S(2)}) collective-permute-start(bf16[1,128,4096]{2,1,0:T(8,128)(2,1)S(1)} %collective-permute-done.3.refs_3_), channel_id=1, source_target_pairs={{0,1},{1,2},{2,3},{3,0},{4,5},{5,6},{6,7},{7,4},{8,9},{9,10},{10,1... | collective-permute-start | bytes 3145736 | tf_op jit(solution)/shard_map/ppermute | solution.py:29
  77.3 42.1 %collective-permute-start.11 = (bf16[1,128,4096]{2,1,0:T(8,128)(2,1)}, bf16[1,128,4096]{2,1,0:T(8,128)(2,1)}, u32[]{:S(2)}, u32[]{:S(2)}) collective-permute-start(bf16[1,128,4096]{2,1,0:T(8,128)(2,1)} %collective-permute-done.refs_12_), channel_id=1, source_target_pairs={{0,4},{1,5},{2,6},{3,7},{4,8},{5,9},{6,10},{7,11},{8,12},{9,13},{1... | collective-permute-start | bytes 3145736 | tf_op jit(solution)/shard_map/ppermute | solution.py:29
  79.0 43.3 %collective-permute-start.12 = (bf16[1,128,4096]{2,1,0:T(8,128)(2,1)S(1)}, bf16[1,128,4096]{2,1,0:T(8,128)(2,1)}, u32[]{:S(2)}, u32[]{:S(2)}) collective-permute-start(bf16[1,128,4096]{2,1,0:T(8,128)(2,1)S(1)} %collective-permute-done.3.refs_3_), channel_id=1, source_target_pairs={{0,12},{1,13},{2,14},{3,15},{4,0},{5,1},{6,2},{7,3},{8,4},{9,5},{1... | collective-permute-start | bytes 3145736 | tf_op jit(solution)/shard_map/ppermute | solution.py:29
  96.7 25.5 %collective-permute-start.13 = (bf16[4,896,128]{2,1,0:T(8,128)(2,1)}, bf16[4,896,128]{2,1,0:T(8,128)(2,1)}, u32[]{:S(2)}, u32[]{:S(2)}) collective-permute-start(bf16[4,896,128]{2,1,0:T(8,128)(2,1)} %pad_maximum_fusion), channel_id=1, source_target_pairs={{0,1},{1,2},{2,3},{3,0},{4,5},{5,6},{6,7},{7,4},{8,9},{9,10},{10,1... | collective-permute-start | bytes 2752520 | tf_op jit(solution)/shard_map/ppermute | solution.py:29
  99.8 39.0 %collective-permute-start.14 = (bf16[1,128,4096]{2,1,0:T(8,128)(2,1)S(1)}, bf16[1,128,4096]{2,1,0:T(8,128)(2,1)}, u32[]{:S(2)}, u32[]{:S(2)}) collective-permute-start(bf16[1,128,4096]{2,1,0:T(8,128)(2,1)S(1)} %collective-permute-done.3.refs_3_), channel_id=1, source_target_pairs={{0,4},{1,5},{2,6},{3,7},{4,8},{5,9},{6,10},{7,11},{8,12},{9,13},{1... | collective-permute-start | bytes 3145736 | tf_op jit(solution)/shard_map/ppermute | solution.py:29
  101.3 43.4 %collective-permute-start.15 = (bf16[1,128,4096]{2,1,0:T(8,128)(2,1)}, bf16[1,128,4096]{2,1,0:T(8,128)(2,1)}, u32[]{:S(2)}, u32[]{:S(2)}) collective-permute-start(bf16[1,128,4096]{2,1,0:T(8,128)(2,1)} %collective-permute-done.9.refs_15_), channel_id=1, source_target_pairs={{0,12},{1,13},{2,14},{3,15},{4,0},{5,1},{6,2},{7,3},{8,4},{9,5},{1... | collective-permute-start | bytes 3145736 | tf_op jit(solution)/shard_map/ppermute | solution.py:29
  105.8 19.4 %all-to-all-start.1 = ((f32[16,32,128]{2,1,0:T(8,128)}), f32[16,32,128]{2,1,0:T(8,128)S(1)}, u32[]{:S(2)}, u32[]{:S(2)}) async-start(f32[16,32,128]{2,1,0:T(8,128)} %broadcast_in_dim.13), calls=%async_computation.1 | async-start | bytes 524288 | tf_op jit(solution)/shard_map/all_to_all | solution.py:137
  122.2 42.3 %collective-permute-start.16 = (bf16[1,128,4096]{2,1,0:T(8,128)(2,1)S(1)}, bf16[1,128,4096]{2,1,0:T(8,128)(2,1)}, u32[]{:S(2)}, u32[]{:S(2)}) collective-permute-start(bf16[1,128,4096]{2,1,0:T(8,128)(2,1)S(1)} %collective-permute-done.10.refs_4_), channel_id=1, source_target_pairs={{0,12},{1,13},{2,14},{3,15},{4,0},{5,1},{6,2},{7,3},{8,4},{9,5},{1... | collective-permute-start | bytes 3145736 | tf_op jit(solution)/shard_map/ppermute | solution.py:29
  125.1 42.5 %collective-permute-start.17 = (bf16[4,896,128]{2,1,0:T(8,128)(2,1)}, bf16[4,896,128]{2,1,0:T(8,128)(2,1)S(1)}, u32[]{:S(2)}, u32[]{:S(2)}) collective-permute-start(bf16[4,896,128]{2,1,0:T(8,128)(2,1)} %pad_maximum_fusion.1), channel_id=1, source_target_pairs={{0,2},{1,3},{2,0},{3,1},{4,6},{5,7},{6,4},{7,5},{8,10},{9,11},{10,... | collective-permute-start | bytes 2752520 | tf_op jit(solution)/shard_map/ppermute | solution.py:29
  125.1 50.8 %collective-permute-start.19 = (bf16[1,128,4096]{2,1,0:T(8,128)(2,1)S(1)}, bf16[1,128,4096]{2,1,0:T(8,128)(2,1)}, u32[]{:S(2)}, u32[]{:S(2)}) collective-permute-start(bf16[1,128,4096]{2,1,0:T(8,128)(2,1)S(1)} %collective-permute-done.10.refs_4_), channel_id=1, source_target_pairs={{0,4},{1,5},{2,6},{3,7},{4,8},{5,9},{6,10},{7,11},{8,12},{9,13},{1... | collective-permute-start | bytes 3145736 | tf_op jit(solution)/shard_map/ppermute | solution.py:29
  144.7 36.6 %collective-permute-start.18 = (bf16[1,128,4096]{2,1,0:T(8,128)(2,1)}, bf16[1,128,4096]{2,1,0:T(8,128)(2,1)S(1)}, u32[]{:S(2)}, u32[]{:S(2)}) collective-permute-start(bf16[1,128,4096]{2,1,0:T(8,128)(2,1)} %collective-permute-done.14.refs_4_), channel_id=1, source_target_pairs={{0,4},{1,5},{2,6},{3,7},{4,8},{5,9},{6,10},{7,11},{8,12},{9,13},{1... | collective-permute-start | bytes 3145736 | tf_op jit(solution)/shard_map/ppermute | solution.py:29
  146.3 1.2 copy-start.3
  147.5 1.2 copy-start.5
  148.6 1.2 copy-start.6
  149.9 17.6 %copy-start.7 = (bf16[1,896,128]{2,1,0:T(8,128)(2,1)S(1)}, bf16[1,896,128]{2,1,0:T(8,128)(2,1)}, u32[]{:S(2)}) copy-start(bf16[1,896,128]{2,1,0:T(8,128)(2,1)} %get-tuple-element.165) | copy-start | bytes 688132
  149.9 17.6 %copy-start.8 = (bf16[1,896,128]{2,1,0:T(8,128)(2,1)S(1)}, bf16[1,896,128]{2,1,0:T(8,128)(2,1)}, u32[]{:S(2)}) copy-start(bf16[1,896,128]{2,1,0:T(8,128)(2,1)} %get-tuple-element.159) | copy-start | bytes 688132
  149.9 17.6 %copy-start.9 = (bf16[1,896,128]{2,1,0:T(8,128)(2,1)S(1)}, bf16[1,896,128]{2,1,0:T(8,128)(2,1)}, u32[]{:S(2)}) copy-start(bf16[1,896,128]{2,1,0:T(8,128)(2,1)} %get-tuple-element.162) | copy-start | bytes 688132
  149.9 17.6 %copy-start.10 = (bf16[1,896,128]{2,1,0:T(8,128)(2,1)S(1)}, bf16[1,896,128]{2,1,0:T(8,128)(2,1)}, u32[]{:S(2)}) copy-start(bf16[1,896,128]{2,1,0:T(8,128)(2,1)} %get-tuple-element.167) | copy-start | bytes 688132
  164.5 24.5 %collective-permute-start.21 = (bf16[1,128,4096]{2,1,0:T(8,128)(2,1)}, bf16[1,128,4096]{2,1,0:T(8,128)(2,1)S(1)}, u32[]{:S(2)}, u32[]{:S(2)}) collective-permute-start(bf16[1,128,4096]{2,1,0:T(8,128)(2,1)} %collective-permute-done.16.refs_7_), channel_id=1, source_target_pairs={{0,12},{1,13},{2,14},{3,15},{4,0},{5,1},{6,2},{7,3},{8,4},{9,5},{1... | collective-permute-start | bytes 3145736 | tf_op jit(solution)/shard_map/ppermute | solution.py:29
  167.6 21.4 %collective-permute-start.20 = (bf16[4,896,128]{2,1,0:T(8,128)(2,1)S(1)}, bf16[4,896,128]{2,1,0:T(8,128)(2,1)S(1)}, u32[]{:S(2)}, u32[]{:S(2)}) collective-permute-start(bf16[4,896,128]{2,1,0:T(8,128)(2,1)S(1)} %pad_maximum_fusion.2), channel_id=1, source_target_pairs={{0,3},{1,0},{2,1},{3,2},{4,7},{5,4},{6,5},{7,6},{8,11},{9,8},{10,9... | collective-permute-start | bytes 2752520 | tf_op jit(solution)/shard_map/ppermute | solution.py:29
